TPU v7x, 128 devices: a whole 4x4x4 slice. The times are simulated.
128 devices in a mesh: gy: 16 (over x, z_lo, core), gz: 8 (over y, z_hi).
Axes of the slice: x: 4, y: 4, z: 4 (z_hi: 2, z_lo: 2; z = z_hi * 2 + z_lo), core: 2. Of those that a mesh axis runs over, the one named last changes fastest.
Arguments:
- field: bfloat16 [32, 2, 2048, 2048], P(None, None, 'gy', 'gz'), may hold values from -6 to 6
- spec_weight: bfloat16 [4096, 2048], P(('gy', 'gz')), may hold values from -4 to 4
- point_weight: bfloat16 [32, 32], replicated, may hold values from -1 to 1
- bias: bfloat16 [32], replicated, may hold values from -3 to 3
- cotangent: bfloat16 [32, 2, 2048, 2048], P(None, None, 'gy', 'gz'), may hold values from -16 to 16
Outputs:
- output: bfloat16 [32, 2, 2048, 2048], P(None, None, 'gy', 'gz')
- grad_input: bfloat16 [32, 2, 2048, 2048], P(None, None, 'gy', 'gz')
- grad_spec: float32 [4096, 2048], P(('gy', 'gz'))
- grad_point: float32 [32, 32], replicated
- grad_bias: float32 [32], replicated
All inputs are finite; a program needn't handle non-finite values.
Results may differ from a plain program's by a relative error of at most 0.008.
Values may be sent and summed in bfloat16 or wider, within the bound.
A program may use at most 128 MiB of HBM per device.

v0:
```python
import math

import jax
import jax.numpy as jnp
from jax import lax
from jax.sharding import PartitionSpec as P

Y = 2048
Z = 2048
KY = 64
KZ = 64


highest = lax.Precision.HIGHEST


def wave_table(freq, position, length):
    turns = freq[:, None] * position[None, :] % length
    angle = turns.astype(jnp.float32) * (2.0 * math.pi / length)
    return (jnp.cos(angle), jnp.sin(angle))


def kept_freq(index, length, kept):
    return jnp.where(index < kept // 2, index, length - kept + index)


def z_forward_table(z_position):
    z_cosine, z_sine = wave_table(jnp.arange(KZ, dtype=jnp.int32), z_position, Z)
    return jnp.concatenate([z_cosine.T, -z_sine.T], axis=1)


def z_inverse_table(z_position):
    z_cosine, z_sine = wave_table(jnp.arange(KZ, dtype=jnp.int32), z_position, Z)
    return jnp.concatenate([z_cosine, -z_sine], axis=0)


def forward_rows(spread, y_cosine, y_sine):
    z_real = spread[..., :KZ]
    z_imag = spread[..., KZ:]
    real_part = jnp.einsum("ky,cxyq->kqcx", y_cosine, z_real, precision=highest) + jnp.einsum(
        "ky,cxyq->kqcx", y_sine, z_imag, precision=highest
    )
    imag_part = jnp.einsum("ky,cxyq->kqcx", y_cosine, z_imag, precision=highest) - jnp.einsum(
        "ky,cxyq->kqcx", y_sine, z_real, precision=highest
    )
    return jnp.stack([real_part, imag_part], axis=2)


def inverse_rows(piece, y_cosine, y_sine):
    piece_real = piece[:, :, 0]
    piece_imag = piece[:, :, 1]
    sum_real = jnp.einsum("ky,kqcx->cxyq", y_cosine, piece_real, precision=highest) - jnp.einsum(
        "ky,kqcx->cxyq", y_sine, piece_imag, precision=highest
    )
    sum_imag = jnp.einsum("ky,kqcx->cxyq", y_cosine, piece_imag, precision=highest) + jnp.einsum(
        "ky,kqcx->cxyq", y_sine, piece_real, precision=highest
    )
    return jnp.concatenate([sum_real, sum_imag], axis=-1)


def local(field, spec_weight, point_weight, bias, cotangent):
    channels = field.shape[0]
    planes = field.shape[1]
    rows_local = field.shape[2]
    cols_local = field.shape[3]
    y_position = lax.axis_index("gy") * rows_local + jnp.arange(rows_local, dtype=jnp.int32)
    z_position = lax.axis_index("gz") * cols_local + jnp.arange(cols_local, dtype=jnp.int32)
    scale = 1.0 / math.sqrt(Y * Z)

    def y_table(count):
        return wave_table(kept_freq(jnp.arange(count, dtype=jnp.int32), Y, KY), y_position, Y)

    def to_modes(data):
        spread = jnp.einsum(
            "cxyz,zq->cxyq",
            data.astype(jnp.float32),
            z_forward_table(z_position),
            precision=highest,
        )
        y_cosine, y_sine = y_table(KY)
        partial_all = (forward_rows(spread, y_cosine, y_sine) * scale).reshape(KY * KZ, -1)
        owned = lax.psum_scatter(partial_all, ("gy", "gz"), scatter_dimension=0, tiled=True)
        return owned.reshape(-1, 2, channels, planes)

    def to_grid(modes):
        gathered = lax.all_gather(
            modes.reshape(modes.shape[0], -1), ("gy", "gz"), axis=0, tiled=True
        )
        gathered = gathered.reshape(KY, KZ, 2, channels, planes)
        y_cosine, y_sine = y_table(KY)
        spread = inverse_rows(gathered, y_cosine, y_sine)
        return jnp.einsum(
            "cxyq,qz->cxyz", spread, z_inverse_table(z_position), precision=highest
        ) * (2.0 * scale)

    weights = spec_weight.astype(jnp.float32).reshape(-1, 2, channels, channels)
    w_real = weights[:, 0]
    w_imag = weights[:, 1]
    spectrum = to_modes(field)
    spec_real = spectrum[:, 0]
    spec_imag = spectrum[:, 1]
    mixed_real = jnp.einsum("mio,mix->mox", w_real, spec_real, precision=highest) - jnp.einsum(
        "mio,mix->mox", w_imag, spec_imag, precision=highest
    )
    mixed_imag = jnp.einsum("mio,mix->mox", w_real, spec_imag, precision=highest) + jnp.einsum(
        "mio,mix->mox", w_imag, spec_real, precision=highest
    )
    spectral = to_grid(jnp.stack([mixed_real, mixed_imag], axis=1))
    pointwise = jnp.einsum("oi,ixyz->oxyz", point_weight, field, preferred_element_type=jnp.float32)
    pre = spectral + pointwise + bias.astype(jnp.float32)[:, None, None, None]
    output = jax.nn.gelu(pre, approximate=False).astype(jnp.bfloat16)
    slope = 0.5 * (1.0 + jax.scipy.special.erf(pre / math.sqrt(2.0))) + pre * jnp.exp(
        -0.5 * pre * pre
    ) / math.sqrt(2.0 * math.pi)
    grad_pre = (cotangent.astype(jnp.float32) * slope).astype(jnp.bfloat16)
    dual = to_modes(grad_pre) * 2.0
    dual_real = dual[:, 0]
    dual_imag = dual[:, 1]
    grad_w_real = jnp.einsum("mox,mix->mio", dual_real, spec_real, precision=highest) + jnp.einsum(
        "mox,mix->mio", dual_imag, spec_imag, precision=highest
    )
    grad_w_imag = jnp.einsum("mox,mix->mio", dual_imag, spec_real, precision=highest) - jnp.einsum(
        "mox,mix->mio", dual_real, spec_imag, precision=highest
    )
    grad_spec = jnp.stack([grad_w_real, grad_w_imag], axis=1).reshape(weights.shape[0], -1)
    back_real = jnp.einsum("mio,mox->mix", w_real, dual_real, precision=highest) + jnp.einsum(
        "mio,mox->mix", w_imag, dual_imag, precision=highest
    )
    back_imag = jnp.einsum("mio,mox->mix", w_real, dual_imag, precision=highest) - jnp.einsum(
        "mio,mox->mix", w_imag, dual_real, precision=highest
    )
    spectral_back = to_grid(jnp.stack([back_real, back_imag], axis=1)) * 0.5
    point_back = jnp.einsum(
        "oi,oxyz->ixyz", point_weight, grad_pre, preferred_element_type=jnp.float32
    )
    grad_input = (spectral_back + point_back).astype(jnp.bfloat16)
    point_term = jnp.einsum("oxyz,ixyz->oi", grad_pre, field, preferred_element_type=jnp.float32)
    bias_term = jnp.sum(grad_pre, axis=(1, 2, 3), dtype=jnp.float32)
    point_total, bias_total = lax.psum((point_term, bias_term), ("gy", "gz"))
    factor = 1.0 / math.sqrt(planes * Y * Z)
    return (output, grad_input, grad_spec, point_total * factor, bias_total * factor)


def solution(mesh):
    in_specs = (
        P(None, None, "gy", "gz"),
        P(("gy", "gz"), None),
        P(),
        P(),
        P(None, None, "gy", "gz"),
    )
    out_specs = (
        P(None, None, "gy", "gz"),
        P(None, None, "gy", "gz"),
        P(("gy", "gz"), None),
        P(),
        P(),
    )
    return jax.shard_map(local, mesh=mesh, in_specs=in_specs, out_specs=out_specs, check_vma=False)
```

profile of v0, /device:TPU:0, one launch (start us, length us, event | category | flops | bytes accessed | tf_op | source)
XLA Modules:
  0.0 2052.5 jit_solution(2421295069633260268)
XLA Ops:
  7.6 6.1 convolution_bitcast_fusion
  17.7 2.1 subtract_bitcast_fusion.3
  19.8 2.1 add_bitcast_fusion.3
  21.9 2.5 maximum_multiply_fusion
  24.4 5.6 copy.35
  30.1 3.5 mul.183
  36.1 643.1 %reduce-scatter.7.cloned.1.call-done = f32[32,128]{1,0:T(8,128)} async-done(((f32[4096,128]{1,0:T(8,128)}), f32[32,128]{1,0:T(8,128)}) %reduce-scatter.7.cloned.1.call-update) | async-done | bytes 16400
  682.7 8.0 fusion.31
  690.8 286.2 %all-gather.3.cloned.1.call-done = f32[4096,128]{1,0:T(8,128)} async-done(((f32[32,128]{1,0:T(8,128)}), f32[4096,128]{1,0:T(8,128)}) %all-gather.3.cloned.1.call-update) | async-done | bytes 2097168 | tf_op jit(solution)/shard_map/all_gather | solution.py:86
  978.9 3.0 reshape.62
  982.0 5.3 fusion.37
  987.3 3.5 fusion.38
  990.8 3.5 add_bitcast_fusion.2
  994.3 16.3 subtract_bitcast_fusion.2
  1010.6 34.8 %convert_reduce_fusion = (f32[32]{0:T(128)S(1)}, bf16[32,2,128,256]{3,2,1,0:T(8,128)(2,1)S(1)}, bf16[32,2,128,256]{3,2,1,0:T(8,128)(2,1)}) fusion(bf16[32,2,128,256]{3,2,1,0:T(8,128)(2,1)S(1)} %copy-done.5, f32[32]{0:T(128)S(1)} %convert_element_type.40, f32[32,2,128,256]{3,0,2,1:T(8,128)S(1)} %bitcast.223, f32[64,256]{1,0:T(8,128)S(1)} %get-tuple-element.15, ...), kind=kOutput, calls=%fused_computation.15 | convolution fusion | flops 3392176128 | bytes 25297152 | tf_op jit(solution)/shard_map/cxyq,qz->cxyz/dot_general | solution.py:92
  1045.4 4.2 fusion.84
  1053.7 2.1 subtract_bitcast_fusion.1
  1055.8 2.1 add_bitcast_fusion.1
  1057.9 2.5 maximum_multiply_fusion.1
  1060.4 5.7 copy.48
  1066.1 3.9 mul.200
  1071.9 641.9 %reduce-scatter.9.cloned.1.call-done = f32[32,128]{1,0:T(8,128)} async-done(((f32[4096,128]{1,0:T(8,128)}), f32[32,128]{1,0:T(8,128)}) %reduce-scatter.9.cloned.1.call-update) | async-done | bytes 16400
  1717.7 12.2 fusion.75
  1729.9 62.8 %all-reduce = (f32[32,32]{1,0:T(8,128)S(1)}, f32[32]{0:T(128)S(1)}) all-reduce(f32[32,32]{1,0:T(8,128)S(1)} %fusion.75, f32[32]{0:T(128)S(1)} %get-tuple-element.7), channel_id=1, replica_groups=mesh['gy'=16,'gz'=8] {'gy','gz'}, use_global_device_ids=true, to_apply=%region_2.3 | all-reduce | flops 1056 | bytes 8448 | tf_op jit(solution)/shard_map/psum | solution.py:139
  1793.8 8.1 fusion.28
  1807.4 204.3 %all-gather.5.cloned.1.call-done = f32[4096,128]{1,0:T(8,128)} async-done(((f32[32,128]{1,0:T(8,128)}), f32[4096,128]{1,0:T(8,128)}) %all-gather.5.cloned.1.call-update) | async-done | bytes 2097168 | tf_op jit(solution)/shard_map/all_gather | solution.py:86
  2013.6 3.2 reshape.64
  2016.8 5.3 fusion.41
  2022.2 3.5 fusion.42
  2025.7 3.6 add_bitcast_fusion
  2029.3 3.9 subtract_bitcast_fusion
  2033.1 12.4 fusion.9
  (79 shorter events, 30.8 us)
Async XLA Ops:
  7.2 675.6 %copy-start = (bf16[32,32]{1,0:T(8,128)(2,1)S(1)}, bf16[32,32]{1,0:T(8,128)(2,1)}, u32[]{:S(2)}) copy-start(bf16[32,32]{1,0:T(8,128)(2,1)} %param.7) | copy-start | bytes 6148
  7.2 672.0 %reduce-scatter.7.cloned.1.call-start = ((), (), s32[]{:S(2)}) async-start(), calls=%async_computation.4 | async-start | bytes 2113536
  33.6 2.2 copy-start.4
  33.6 648.8 %copy-start.6 = (bf16[32]{0:T(256)(128)(2,1)S(1)}, bf16[32]{0:T(256)(128)(2,1)}, u32[]{:S(2)}) copy-start(bf16[32]{0:T(256)(128)(2,1)} %param.8) | copy-start | bytes 196
  35.5 941.6 %all-gather.3.cloned.1.call-start = ((), (), s32[]{:S(2)}) async-start(), calls=%async_computation.2 | async-start | bytes 2113536 | tf_op jit(solution)/shard_map/all_gather | solution.py:86
  682.4 1031.4 %reduce-scatter.9.cloned.1.call-start = ((), (), s32[]{:S(2)}) async-start(), calls=%async_computation.5 | async-start | bytes 2113536
  982.0 5.3 copy-start.2
  987.3 23.3 %slice-start.2 = ((s8[8388608]{0:T(1024)(128)(4,1)}), s8[4194304]{0:T(1024)(128)(4,1)S(1)}, s32[]{:S(2)}) async-start(s8[8388608]{0:T(1024)(128)(4,1)} %bitcast.222), calls=%async_computation.8 | async-start | bytes 8388608
  990.8 19.8 slice-start.3
  994.3 16.3 copy-start.5
  1045.4 4.2 copy-start.3
  1071.8 939.8 %all-gather.5.cloned.1.call-start = ((), (), s32[]{:S(2)}) async-start(), calls=%async_computation.3 | async-start | bytes 2113536 | tf_op jit(solution)/shard_map/all_gather | solution.py:86
  2016.8 5.3 copy-start.1
  2022.1 11.0 slice-start
  2025.6 7.5 slice-start.1
Sparse Core Ops, SparseCore 0:
  35.6 643.5 reduce-scatter.6
  682.5 294.4 all-gather.2
  1072.0 641.7 reduce-scatter.8
  1717.8 293.8 all-gather.4
where the time goes:
time: 2060 us; the launch traced here: 2050 us
  waiting for transfers between devices  1780 us (86%)
  matrix products  155 us (8%)
  blocking collectives  62.8 us (3%)
  local copies, waits for them, and re-layouts  37.7 us (2%)
    unnamed x6, waiting for transfers between devices  1280 us
    all_gather x2, waiting for transfers between devices, to_grid(): lax.all_gather(modes.reshape(modes.shape[0], -1), ('gy', 'gz'), axis=0, t...  491 us
    psum x1, blocking collectives, local(): point_total, bias_total = lax.psum((point_term, bias_term), ('gy', 'gz'))  62.8 us
    dot_general x2, matrix products, to_grid(): jnp.einsum('cxyq,qz->cxyz', spread, z_inverse_table(z_position), precisio...  47.2 us
  transfers between devices with their start and end apart: 4, of which 4 were waited for; matrix products, arithmetic and copies ran while one was open for 2% of the time, Pallas kernels for 0%

commit v1 on v0

v1 whole, which is shorter than its diff:
```python
import functools
import math

import jax
import jax.numpy as jnp
import numpy as np
from jax import lax
from jax.experimental import pallas as pl
from jax.experimental.pallas import tpu as pltpu

P = jax.sharding.PartitionSpec
BF = jnp.bfloat16
F32 = jnp.float32

C = 32
X = 2
Y = 2048
Z = 2048
K = 64
ROWS = 128
COLS = 256
G = 16
NG = ROWS // G

MESH = pl.DeviceIdType.MESH


def row_order():
    order = []
    for core in range(2):
        for cx in range(4):
            for cy in range(4):
                for lo in range(2):
                    order.append(cx * 16 + lo * 8 + core * 4 + cy)
    return np.array(order)


def make_tables():
    j = row_order()
    fy = np.where(j < K // 2, j, Y - K + j)
    y = np.arange(Y)
    ang_y = 2.0 * np.pi * ((fy[:, None] * y[None, :]) % Y) / Y
    z = np.arange(Z)
    ang_z = 2.0 * np.pi * ((np.arange(K)[:, None] * z[None, :]) % Z) / Z
    cy, sy = np.cos(ang_y), np.sin(ang_y)
    cz, sz = np.cos(ang_z), np.sin(ang_z)
    zf = np.concatenate([cz, -sz, -sz, -cz], axis=0)
    zf = zf.reshape(4 * K, Z // COLS, COLS).transpose(1, 0, 2)
    yf = np.stack([cy, sy], axis=0).reshape(2, K, Y // ROWS, ROWS)
    yf = yf.transpose(2, 1, 0, 3).reshape(Y // ROWS, K, 2 * ROWS)
    yi = np.stack([cy, sy], axis=0).reshape(2, K, Y // ROWS, ROWS)
    yi = yi.transpose(2, 0, 3, 1).reshape(Y // ROWS, 2 * ROWS, K)
    bf = lambda a: np.ascontiguousarray(a).astype(jnp.bfloat16)
    scale = 1.0 / math.sqrt(Y * Z)
    return (
        bf(zf.transpose(0, 2, 1)),
        bf(zf),
        bf(yf * scale),
        bf(yi * (2.0 * scale)),
    )


def make_spreads():
    lane = np.arange(C * C)
    rows = np.arange(C)[:, None]
    over_o = (lane[None, :] // C == rows).astype(np.float32)
    over_i = (lane[None, :] % C == rows).astype(np.float32)
    return over_o.astype(jnp.bfloat16), over_i.astype(jnp.bfloat16)


def dot(a, b):
    return jnp.dot(a, b, preferred_element_type=F32)


def dot_nt(a, b):
    return lax.dot_general(a, b, (((1,), (1,)), ((), ())), preferred_element_type=F32)


def split(v):
    hi = v.astype(BF)
    return hi, (v - hi.astype(F32)).astype(BF)


def rows_to_modes(get_rows, yf_ref, wide, part):
    @pl.loop(0, C // 4)
    def _(n):
        for e in range(4):
            c = n * 4 + e
            d = get_rows(c)
            wide[pl.ds(c, K, stride=C), :] = dot(yf_ref[:, :ROWS], d[:, : 2 * K]) + dot(
                yf_ref[:, ROWS:], d[:, 2 * K :]
            )

    @pl.loop(0, 8)
    def _(n):
        at = pl.multiple_of(n * (K * C // 8), K * C // 8)
        part[pl.ds(n * (K // 8), K // 8)] = (
            wide[pl.ds(at, K * C // 8), :].astype(BF).reshape(K // 8, C, 2 * K)
        )


def modes_to_rows(part, yi_ref, wide, spread):
    @pl.loop(0, 8)
    def _(n):
        at = pl.multiple_of(n * (K * C // 8), K * C // 8)
        wide[pl.ds(at, K * C // 8), :] = (
            part[pl.ds(n * (K // 8), K // 8)].astype(F32).reshape(K * C // 8, 2 * K)
        )

    @pl.loop(0, C // 4)
    def _(n):
        for e in range(4):
            c = n * 4 + e
            m = wide[pl.ds(c, K, stride=C), :].astype(BF)
            r = dot(yi_ref[...], m).astype(BF)
            spread[c, :, : 2 * K] = r[:ROWS]
            spread[c, :, 2 * K :] = r[ROWS:]


def first_kernel(field, zf, yf, out, buf, rows, wide, sems):
    copies = [pltpu.make_async_copy(field.at[:, x], buf.at[x], sems.at[x]) for x in range(X)]
    for copy in copies:
        copy.start()
    for x in range(X):
        copies[x].wait()

        @pl.loop(0, C // 2)
        def _(n):
            f = buf[x, pl.ds(n * 2, 2)].reshape(2 * ROWS, COLS)
            rows[pl.ds(n * 2, 2)] = dot(f, zf[...]).astype(BF).reshape(2, ROWS, 4 * K)

        rows_to_modes(lambda c: rows[c], yf, wide, out.at[x])


def places():
    gy, gz = lax.axis_index("gy"), lax.axis_index("gz")
    return dict(x=gy // 4, lo=gy // 2 % 2, core=gy % 2, y=gz // 2, hi=gz % 2)


def device(at, **other):
    at = dict(at, **other)
    return {
        "gy": at["x"] * 4 + at["lo"] * 2 + at["core"],
        "gz": at["y"] * 2 + at["hi"],
    }


def turned(at, axis, step):
    return lax.rem(at[axis] + step, 4)


def z_partners(at):
    return [
        dict(hi=at["hi"], lo=1 - at["lo"]),
        dict(hi=1 - at["hi"], lo=at["lo"]),
        dict(hi=1 - at["hi"], lo=1 - at["lo"]),
    ]


def greet(at):
    barrier = pltpu.get_barrier_semaphore()
    partners = [device(at, core=1 - at["core"])]
    for axis in ("x", "y"):
        partners += [device(at, **{axis: turned(at, axis, s)}) for s in (1, 2, 3)]
    partners += [device(at, **p) for p in z_partners(at)]
    for partner in partners:
        pl.semaphore_signal(barrier, inc=1, device_id=partner, device_id_type=MESH)
    pl.semaphore_wait(barrier, len(partners))


AXES = (("x", "y"), ("y", "x"))


def send(src, dst, sems, n, to):
    send_sem, recv_sem = sems
    copy = pltpu.make_async_remote_copy(
        src_ref=src,
        dst_ref=dst,
        send_sem=send_sem.at[n],
        recv_sem=recv_sem.at[n],
        device_id=to,
        device_id_type=MESH,
    )
    copy.start()
    return copy


def scatter_core(at, p, part, b, sems):
    other = 1 - at["core"]
    return [send(part.at[p, other], b["r1"].at[p], sems, 18 * p, device(at, core=other))]


def scatter_first(at, p, part, b, sems):
    me = at["core"]
    b["s1"][p] = (part[p, me].astype(F32) + b["r1"][p].astype(F32)).astype(BF)
    axis = AXES[p][0]
    copies = []
    for s in (1, 2, 3):
        to = turned(at, axis, s)
        src = b["s1"].at[p, to] if axis == "x" else b["s1"].at[p, :, to]
        copies.append(
            send(src, b["r2"].at[p, s - 1], sems, 18 * p + s, device(at, **{axis: to}))
        )
    return copies


def scatter_second(at, p, part, b, sems):
    axis, second = AXES[p]
    own = b["s1"][p, at["x"]] if axis == "x" else b["s1"][p, :, at["y"]]
    total = own.astype(F32)
    for s in range(3):
        total = total + b["r2"][p, s].astype(F32)
    b["s2"][p] = total.astype(BF)
    copies = []
    for s in (1, 2, 3):
        to = turned(at, second, s)
        copies.append(
            send(
                b["s2"].at[p, to],
                b["r3"].at[p, s - 1],
                sems,
                18 * p + 3 + s,
                device(at, **{second: to}),
            )
        )
    return copies


def scatter_last(at, p, part, b, sems):
    second = AXES[p][1]
    total = b["s2"][p, at[second]].astype(F32)
    for s in range(3):
        total = total + b["r3"][p, s].astype(F32)
    b["s3"][p] = total
    b["s3h"][p] = total.astype(BF)
    copies = []
    for n, to in enumerate(z_partners(at)):
        copies.append(
            send(
                b["s3h"].at[p, to["lo"]],
                b["r4"].at[p, n],
                sems,
                18 * p + 7 + n,
                device(at, **to),
            )
        )
    return copies


def scatter_total(at, p, b):
    total = b["s3"][p, at["lo"]]
    for n in range(3):
        total = total + b["r4"][p, n].astype(F32)
    return total


def gather_first(at, p, modes, sems):
    here = modes.at[p, at["core"], at["x"], at["y"], at["lo"]]
    return [send(here, here, sems, 18 * p + 10, device(at, lo=1 - at["lo"]))]


def gather_second(at, p, modes, sems):
    here = modes.at[p, at["core"], at["x"], at["y"]]
    axis = AXES[p][1]
    return [
        send(here, here, sems, 18 * p + 10 + s, device(at, **{axis: turned(at, axis, s)}))
        for s in (1, 2, 3)
    ]


def gather_third(at, p, modes, sems):
    axis = AXES[p][0]
    if axis == "x":
        here = modes.at[p, at["core"], at["x"]]
    else:
        here = modes.at[p, at["core"], :, at["y"]]
    return [
        send(here, here, sems, 18 * p + 13 + s, device(at, **{axis: turned(at, axis, s)}))
        for s in (1, 2, 3)
    ]


def gather_core(at, p, modes, sems):
    here = modes.at[p, at["core"]]
    return [send(here, here, sems, 18 * p + 17, device(at, core=1 - at["core"]))]


N_SEMS = 36


def exchange_scratch():
    return dict(
        r1=pltpu.VMEM((X, 4, 4, 2, C, 2 * K), BF),
        s1=pltpu.VMEM((X, 4, 4, 2, C, 2 * K), BF),
        r2=pltpu.VMEM((X, 3, 4, 2, C, 2 * K), BF),
        s2=pltpu.VMEM((X, 4, 2, C, 2 * K), BF),
        r3=pltpu.VMEM((X, 3, 2, C, 2 * K), BF),
        s3=pltpu.VMEM((X, 2, C, 2 * K), F32),
        s3h=pltpu.VMEM((X, 2, C, 2 * K), BF),
        r4=pltpu.VMEM((X, 3, C, 2 * K), BF),
        sends=pltpu.SemaphoreType.DMA((N_SEMS,)),
        recvs=pltpu.SemaphoreType.DMA((N_SEMS,)),
    )


def run_scatter(at, part, b, sems, every):
    flight = [scatter_core(at, p, part, b, sems) for p in range(X)]
    every += flight[0] + flight[1]
    for stage in (scatter_first, scatter_second, scatter_last):
        for p in range(X):
            for copy in flight[p]:
                copy.wait_recv()
            flight[p] = stage(at, p, part, b, sems)
            every += flight[p]
    totals = []
    for p in range(X):
        for copy in flight[p]:
            copy.wait_recv()
        totals.append(scatter_total(at, p, b))
    return totals


def run_gather(at, modes, sems, every):
    flight = [gather_first(at, p, modes, sems) for p in range(X)]
    every += flight[0] + flight[1]
    for stage in (gather_second, gather_third, gather_core):
        for p in range(X):
            for copy in flight[p]:
                copy.wait_recv()
            flight[p] = stage(at, p, modes, sems)
            every += flight[p]
    for p in range(X):
        for copy in flight[p]:
            copy.wait_recv()


def widen(v, table):
    hi, lo = split(v)
    return dot(hi, table) + dot(lo, table)


def narrow(v, table):
    hi, lo = split(v)
    return dot_nt(hi, table) + dot_nt(lo, table)


def put_modes(at, p, modes, real, imag):
    block = jnp.concatenate([real, imag], axis=0).T
    modes[p, at["core"], at["x"], at["y"], at["lo"]] = block.astype(BF)


def mix_kernel(part, weights, over_o, over_i, modes, spec, w_all, b, w_sems):
    at = places()
    greet(at)
    sems = (b["sends"], b["recvs"])
    every = []
    hi = at["hi"]
    w_here = pltpu.make_async_copy(weights, w_all.at[hi], w_sems.at[0])
    w_here.start()
    w_there = pltpu.make_async_remote_copy(
        src_ref=weights,
        dst_ref=w_all.at[hi],
        send_sem=w_sems.at[1],
        recv_sem=w_sems.at[2],
        device_id=device(at, hi=1 - hi),
        device_id_type=MESH,
    )
    w_there.start()
    totals = run_scatter(at, part, b, sems, every)
    w_here.wait()
    w_there.wait()
    w = w_all[...].reshape(K, 2 * C * C).astype(F32)
    w_real, w_imag = w[:, : C * C], w[:, C * C :]
    for p in range(X):
        t = totals[p].T
        spec[p] = t
        s_real = widen(t[:K], over_o[...])
        s_imag = widen(t[K:], over_o[...])
        real = narrow(w_real * s_real - w_imag * s_imag, over_i[...])
        imag = narrow(w_real * s_imag + w_imag * s_real, over_i[...])
        put_modes(at, p, modes, real, imag)
    run_gather(at, modes, sems, every)
    for copy in every:
        copy.wait_send()


def unmix_kernel(
    part, w_all, spec, over_o, over_i, small, modes, grad, small_out, b, grad_all, s_small, r_small, small_sems, grad_sem
):
    at = places()
    greet(at)
    sems = (b["sends"], b["recvs"])
    every = []
    small_send, small_recv = small_sems

    groups = [
        [device(at, core=1 - at["core"])],
        [device(at, x=turned(at, "x", s)) for s in (1, 2, 3)],
        [device(at, y=turned(at, "y", s)) for s in (1, 2, 3)],
        [device(at, **to) for to in z_partners(at)],
    ]

    def small_stage(n):
        base = (0, 1, 4, 7)[n]
        return [
            send(s_small.at[n], r_small.at[base + e], (small_send, small_recv), base + e, to)
            for e, to in enumerate(groups[n])
        ]

    def small_sum(n, copies):
        base = (0, 1, 4, 7)[n]
        total = s_small[n]
        for e, copy in enumerate(copies):
            copy.wait_recv()
            total = total + r_small[base + e]
        s_small[n + 1] = total

    s_small[0] = small[...]
    totals = run_scatter(at, part, b, sems, every)
    w = w_all[...].reshape(K, 2 * C * C).astype(F32)
    w_real, w_imag = w[:, : C * C], w[:, C * C :]
    for p in range(X):
        t = totals[p].T * 2.0
        d_real = widen(t[:K], over_i[...])
        d_imag = widen(t[K:], over_i[...])
        real = narrow(w_real * d_real + w_imag * d_imag, over_o[...])
        imag = narrow(w_real * d_imag - w_imag * d_real, over_o[...])
        put_modes(at, p, modes, real * 0.5, imag * 0.5)
        s_real = widen(spec[p, :K], over_o[...])
        s_imag = widen(spec[p, K:], over_o[...])
        g_real = d_real * s_real + d_imag * s_imag
        g_imag = d_imag * s_real - d_real * s_imag
        if p == 0:
            grad_all[:, : C * C] = g_real
            grad_all[:, C * C :] = g_imag
        else:
            grad_all[:, : C * C] += g_real
            grad_all[:, C * C :] += g_imag
    keep = pl.ds(pl.multiple_of(at["hi"] * (K // 2), K // 2), K // 2)
    grad_out = pltpu.make_async_copy(grad_all.at[keep], grad, grad_sem)
    grad_out.start()
    for n in range(4):
        copies = small_stage(n)
        every += copies
        small_sum(n, copies)
    small_out[...] = s_small[4] * (1.0 / math.sqrt(X * Y * Z))
    run_gather(at, modes, sems, every)
    for copy in every:
        copy.wait_send()
    grad_out.wait()


def gelu_terms(v):
    e = jnp.exp(v * v * -0.5)
    t = 1.0 / (1.0 + jnp.abs(v) * (0.3275911 / math.sqrt(2.0)))
    q = t * (0.5 * 1.061405429) - 0.5 * 1.453152027
    q = q * t + 0.5 * 1.421413741
    q = q * t - 0.5 * 0.284496736
    q = q * t + 0.5 * 0.254829592
    q = q * t * e
    phi = jnp.where(v >= 0.0, 1.0 - q, q)
    return v * phi, phi + v * e * (1.0 / math.sqrt(2.0 * math.pi))


def kron_of(weight, over, same):
    wide = dot_nt(dot(over, weight).astype(BF), over)
    return jnp.where(same, wide, 0.0).astype(BF)


def group_masks():
    a = lax.broadcasted_iota(jnp.int32, (C * G, C * G), 0)
    b = lax.broadcasted_iota(jnp.int32, (C * G, C * G), 1)
    same = lax.rem(a, G) == lax.rem(b, G)
    m = lax.broadcasted_iota(jnp.int32, (C * G, C), 0)
    n = lax.broadcasted_iota(jnp.int32, (C * G, C), 1)
    over = (m // G == n).astype(F32).astype(BF)
    return same, over


def middle_kernel(
    field, cot, modes, point, bias, zf, zi, yf, yi,
    out, gp_out, part, small,
    f_buf, c_buf, spread, rows, o_buf, g_buf, wide, kron, bias_col, acc, bias_acc, sems, out_sems,
):
    f_copies = [pltpu.make_async_copy(field.at[:, x], f_buf.at[x], sems.at[0, x]) for x in range(X)]
    c_copies = [pltpu.make_async_copy(cot.at[:, x], c_buf.at[x], sems.at[1, x]) for x in range(X)]
    for x in range(X):
        f_copies[x].start()
        c_copies[x].start()
    same, over = group_masks()
    kron[...] = kron_of(point[...], over, same)
    bias_col[...] = dot(over, bias[...])
    acc[...] = jnp.zeros_like(acc)
    bias_acc[...] = jnp.zeros_like(bias_acc)
    outs = []
    for x in range(X):
        modes_to_rows(modes.at[x], yi, wide, spread)
        f_copies[x].wait()
        c_copies[x].wait()

        @pl.loop(0, NG)
        def _(g):
            at = pl.ds(pl.multiple_of(g * G, G), G)
            f = f_buf[x, :, at, :].reshape(C * G, COLS)
            pre = dot(spread[:, at, :].reshape(C * G, 4 * K), zi[...])
            pre = pre + dot(kron[...], f) + bias_col[:, :1]
            value, slope = gelu_terms(pre)
            o_buf[x, :, at, :] = value.astype(BF).reshape(C, G, COLS)
            gp = (c_buf[x, :, at, :].reshape(C * G, COLS).astype(F32) * slope).astype(BF)
            g_buf[x, :, at, :] = gp.reshape(C, G, COLS)
            wide_gp = gp.astype(F32)
            bias_acc[...] += wide_gp[:, : COLS // 2] + wide_gp[:, COLS // 2 :]
            acc[...] += dot_nt(gp, f)
            rows[:, at, :] = dot(gp, zf[...]).astype(BF).reshape(C, G, 4 * K)

        outs.append(pltpu.make_async_copy(o_buf.at[x], out.at[:, x], out_sems.at[0, x]))
        outs.append(pltpu.make_async_copy(g_buf.at[x], gp_out.at[:, x], out_sems.at[1, x]))
        outs[-2].start()
        outs[-1].start()
        rows_to_modes(lambda c: rows[c], yf, wide, part.at[x])
    kept = jnp.where(same, acc[...], 0.0).reshape(C, G, C * G).sum(axis=1)
    term = jnp.dot(kept, over.astype(F32), precision=lax.Precision.HIGHEST)
    total = bias_acc[...].reshape(C, G, COLS // 2).sum(axis=1).sum(axis=1, keepdims=True)
    small[:, :C] = term
    small[:, C:] = jnp.broadcast_to(total, (C, 2 * K - C))
    for copy in outs:
        copy.wait()


def last_kernel(gp, modes, point_t, zi, yi, out, g_buf, spread, o_buf, wide, kron, sems, out_sems):
    copies = [pltpu.make_async_copy(gp.at[:, x], g_buf.at[x], sems.at[x]) for x in range(X)]
    for copy in copies:
        copy.start()
    same, over = group_masks()
    kron[...] = kron_of(point_t[...], over, same)
    outs = []
    for x in range(X):
        modes_to_rows(modes.at[x], yi, wide, spread)
        copies[x].wait()

        @pl.loop(0, NG)
        def _(g):
            at = pl.ds(pl.multiple_of(g * G, G), G)
            v = dot(spread[:, at, :].reshape(C * G, 4 * K), zi[...])
            v = v + dot(kron[...], g_buf[x, :, at, :].reshape(C * G, COLS))
            o_buf[x, :, at, :] = v.astype(BF).reshape(C, G, COLS)

        outs.append(pltpu.make_async_copy(o_buf.at[x], out.at[:, x], out_sems.at[x]))
        outs[-1].start()
    for copy in outs:
        copy.wait()


VMEM = pl.BlockSpec(memory_space=pltpu.VMEM)
ANY = pl.BlockSpec(memory_space=pl.ANY)
LIMIT = 56 * 1024 * 1024


def params(collective_id=None):
    if collective_id is None:
        return pltpu.CompilerParams(vmem_limit_bytes=LIMIT)
    return pltpu.CompilerParams(
        vmem_limit_bytes=LIMIT, collective_id=collective_id, has_side_effects=True
    )


def grid_buffer(dtype=BF):
    return pltpu.VMEM((X, C, ROWS, COLS), dtype)


def local(field, spec_weight, point_weight, bias, cotangent):
    gy, gz = lax.axis_index("gy"), lax.axis_index("gz")
    zf_all, zi_all, yf_all, yi_all = make_tables()
    zf = lax.dynamic_index_in_dim(jnp.asarray(zf_all), gz, 0, keepdims=False)
    zi = lax.dynamic_index_in_dim(jnp.asarray(zi_all), gz, 0, keepdims=False)
    yf = lax.dynamic_index_in_dim(jnp.asarray(yf_all), gy, 0, keepdims=False)
    yi = lax.dynamic_index_in_dim(jnp.asarray(yi_all), gy, 0, keepdims=False)
    over_o, over_i = (jnp.asarray(t) for t in make_spreads())
    shape = jax.ShapeDtypeStruct
    flat = (X, K, C, 2 * K)
    deep = (X, 2, 4, 4, 2, C, 2 * K)
    wide = pltpu.VMEM((K * C, 2 * K), F32)
    line = pltpu.VMEM((C, ROWS, 4 * K), BF)
    dma = pltpu.SemaphoreType.DMA

    part = pl.pallas_call(
        first_kernel,
        out_shape=shape(flat, BF),
        in_specs=[ANY, VMEM, VMEM],
        out_specs=VMEM,
        scratch_shapes=[grid_buffer(), line, wide, dma((X,))],
        compiler_params=params(),
        name="field_modes",
    )(field, zf, yf)

    modes, spec, w_all = pl.pallas_call(
        mix_kernel,
        out_shape=(shape(deep, BF), shape((X, 2 * K, C), F32), shape((2, K // 2, 2 * C * C), BF)),
        in_specs=[VMEM] * 4,
        out_specs=[VMEM] * 3,
        scratch_shapes=[exchange_scratch(), dma((3,))],
        compiler_params=params(1),
        name="mix_modes",
    )(part.reshape(deep), spec_weight, over_o, over_i)

    bias_in = jnp.broadcast_to(bias[:, None], (C, 2 * K))
    output, grad_pre, part2, small = pl.pallas_call(
        middle_kernel,
        out_shape=(
            shape(field.shape, BF),
            shape(field.shape, BF),
            shape(flat, BF),
            shape((C, 2 * K), F32),
        ),
        in_specs=[ANY, ANY] + [VMEM] * 7,
        out_specs=[ANY, ANY, VMEM, VMEM],
        scratch_shapes=[
            grid_buffer(), grid_buffer(), line, line, grid_buffer(), grid_buffer(), wide,
            pltpu.VMEM((C * G, C * G), BF),
            pltpu.VMEM((C * G, 2 * K), F32),
            pltpu.VMEM((C * G, C * G), F32),
            pltpu.VMEM((C * G, COLS // 2), F32),
            dma((2, X)),
            dma((2, X)),
        ],
        compiler_params=params(),
        name="layer",
    )(field, cotangent, modes.reshape(flat), point_weight, bias_in, zf, zi, yf, yi)

    modes2, grad_spec, small_out = pl.pallas_call(
        unmix_kernel,
        out_shape=(
            shape(deep, BF),
            shape((K // 2, 2 * C * C), F32),
            shape((C, 2 * K), F32),
        ),
        in_specs=[VMEM] * 6,
        out_specs=[VMEM, ANY, VMEM],
        scratch_shapes=[
            exchange_scratch(),
            pltpu.VMEM((K, 2 * C * C), F32),
            pltpu.VMEM((5, C, 2 * K), F32),
            pltpu.VMEM((10, C, 2 * K), F32),
            [dma((10,)), dma((10,))],
            dma,
        ],
        compiler_params=params(2),
        name="unmix_modes",
    )(part2.reshape(deep), w_all, spec, over_o, over_i, small)

    grad_input = pl.pallas_call(
        last_kernel,
        out_shape=shape(field.shape, BF),
        in_specs=[ANY] + [VMEM] * 4,
        out_specs=ANY,
        scratch_shapes=[
            grid_buffer(), line, grid_buffer(), wide,
            pltpu.VMEM((C * G, C * G), BF),
            dma((X,)),
            dma((X,)),
        ],
        compiler_params=params(),
        name="input_gradient",
    )(grad_pre, modes2.reshape(flat), point_weight.T, zi, yi)

    return output, grad_input, grad_spec, small_out[:, :C], small_out[:, C]


def solution(mesh):
    grid = P(None, None, "gy", "gz")
    owned = P(("gy", "gz"), None)
    return jax.shard_map(
        local,
        mesh=mesh,
        in_specs=(grid, owned, P(), P(), grid),
        out_specs=(grid, grid, owned, P(), P()),
        check_vma=False,
    )
```

time: 2060 us -> 155 us (0.08)
  waiting for transfers between devices: 1780 us -> 0 us
  matrix products: 155 us -> 0 us
  Pallas kernels: 0 us -> 144 us
  blocking collectives: 62.8 us -> 0 us
  local copies, waits for them, and re-layouts: 37.7 us -> 9.2 us
    unnamed x6 -> x0, waiting for transfers between devices: 1280 us -> none
    all_gather x2 -> x0, waiting for transfers between devices: 491 us -> none  [to_grid(): lax.all_gather(modes.reshape(modes.shape[0], -1), ('gy', 'gz'), axis=0, t...]
    dot_general x35 -> x0, matrix products: 155 us -> none  [the longest x2 47.2 us: to_grid(): jnp.einsum('cxyq,qz->cxyz', spread, z_inverse_table(z_position), precisio...]
    pallas_call x0 -> x5, Pallas kernels: none -> 144 us  [the longest x1 45.6 us: local(): pl.pallas_call(unmix_kernel, out_shape=(shape(deep, BF), shape((K // 2, 2...]
    psum x1 -> x0, blocking collectives: 62.8 us -> none  [local(): point_total, bias_total = lax.psum((point_term, bias_term), ('gy', 'gz'))]
  transfers between devices with their start and end apart: 4 -> 0, of which waited for: 4 -> 0; matrix products, arithmetic and copies ran while one was open for 2% -> 0% of each run, Pallas kernels for 0% -> 0%
where the time goes in v1:
time: 155 us; the launch traced here: 154 us
  Pallas kernels  144 us (93%)
  local copies, waits for them, and re-layouts  9.2 us (6%)
    pallas_call x1, Pallas kernels, local(): pl.pallas_call(unmix_kernel, out_shape=(shape(deep, BF), shape((K // 2, 2...  45.6 us
    pallas_call x1, Pallas kernels, local(): pl.pallas_call(mix_kernel, out_shape=(shape(deep, BF), shape((X, 2 * K, C...  37.2 us
    pallas_call x1, Pallas kernels, local(): pl.pallas_call(middle_kernel, out_shape=(shape(field.shape, BF), shape(fi...  33.7 us
    pallas_call x1, Pallas kernels, local(): pl.pallas_call(first_kernel, out_shape=shape(flat, BF), in_specs=[ANY, VM...  13.8 us
    pallas_call x1, Pallas kernels, local(): pl.pallas_call(last_kernel, out_shape=shape(field.shape, BF), in_specs=[A...  13.2 us

profile of v1, /device:TPU:0, one launch (start us, length us, event | category | flops | bytes accessed | tf_op | source)
XLA Modules:
  0.0 153.6 jit_solution(8412042210945381587)
XLA Ops:
  0.6 1.3 broadcast_in_dim.2.bias
  2.0 1.4 copy.17
  3.3 1.4 dynamic-slice_bitcast_fusion.3.yf
  4.7 1.5 dynamic-slice_bitcast_fusion.2.yi
  6.1 1.7 %dynamic-slice_bitcast_fusion = (bf16[256,256]{1,0:T(8,128)(2,1)}, bf16[256,256]{1,0:T(8,128)(2,1)}) fusion(bf16[8,256,256]{2,1,0:T(8,128)(2,1)} %constant.39.clone, s32[]{:T(128)S(6)} %select_n.11, bf16[8,256,256]{2,1,0:T(8,128)(2,1)} %constant.38.clone), kind=kLoop, calls=%fused_computation | loop fusion | bytes 524292 | tf_op jit(solution)/shard_map/jit(dynamic_index_in_dim)/squeeze | solution.py:575
  7.8 13.8 %field_modes.1 = bf16[2,64,32,128]{3,2,1,0:T(8,128)(2,1)} custom-call(bf16[32,2,128,256]{3,2,1,0:T(8,128)(2,1)} %field.3, bf16[256,256]{1,0:T(8,128)(2,1)} %get-tuple-element.26.zf, bf16[64,256]{1,0:T(8,128)(2,1)} %dynamic-slice_bitcast_fusion.3.yf), custom_call_target="tpu_custom_call" | custom-call | tf_op jit(solution)/shard_map/field_modes/pallas_call | solution.py:586
  21.7 37.2 %mix_modes.1 = (bf16[2,2,4,4,2,32,128]{6,5,4,3,2,1,0:T(8,128)(2,1)}, f32[2,128,32]{2,1,0:T(8,128)}, bf16[2,32,2048]{2,1,0:T(8,128)(2,1)}) custom-call(bf16[2,2,4,4,2,32,128]{6,5,4,3,2,1,0:T(8,128)(2,1)} %bitcast.14, bf16[32,2048]{1,0:T(8,128)(2,1)} %weights.1, bf16[32,1024]{1,0:T(8,128)(2,1)} %constant.42.clone.over_o, bf16[32,1024]{1,0:T(8,128)(2,1)} %constant.43.clone.over_i), custom_call_target="tpu_custom_call" | custom-call | tf_op jit(solution)/shard_map/mix_modes/pallas_call | solution.py:596
  58.9 33.7 %layer.1 = (bf16[32,2,128,256]{3,2,1,0:T(8,128)(2,1)}, bf16[32,2,128,256]{3,2,1,0:T(8,128)(2,1)}, bf16[2,64,32,128]{3,2,1,0:T(8,128)(2,1)}, f32[32,128]{1,0:T(8,128)}) custom-call(bf16[32,2,128,256]{3,2,1,0:T(8,128)(2,1)} %field.3, bf16[32,2,128,256]{3,2,1,0:T(8,128)(2,1)} %cot.1, bf16[2,64,32,128]{3,2,1,0:T(8,128)(2,1)} %bitcast.15, bf16[32,32]{1,0:T(8,128)(2,1)} %point.1, ...), custom_call_target="tpu_custom_call" | custom-call | tf_op jit(solution)/shard_map/layer/pallas_call | solution.py:607
  92.7 45.6 %unmix_modes.1 = (bf16[2,2,4,4,2,32,128]{6,5,4,3,2,1,0:T(8,128)(2,1)}, f32[32,2048]{1,0:T(8,128)}, f32[32,128]{1,0:T(8,128)}) custom-call(bf16[2,2,4,4,2,32,128]{6,5,4,3,2,1,0:T(8,128)(2,1)} %bitcast.16, bf16[2,32,2048]{2,1,0:T(8,128)(2,1)} %get-tuple-element.19.w_all, f32[2,128,32]{2,1,0:T(8,128)} %get-tuple-element.20.spec, ...), custom_call_target="tpu_custom_call" | custom-call | tf_op jit(solution)/shard_map/unmix_modes/pallas_call | solution.py:630
  138.3 0.0 copy-start.1
  138.3 0.0 copy-start
  138.3 13.2 %input_gradient.1 = bf16[32,2,128,256]{3,2,1,0:T(8,128)(2,1)} custom-call(bf16[32,2,128,256]{3,2,1,0:T(8,128)(2,1)} %get-tuple-element.17.gp, bf16[2,64,32,128]{3,2,1,0:T(8,128)(2,1)} %bitcast.17, bf16[32,32]{1,0:T(8,128)(2,1)} %bitcast.19, bf16[256,256]{1,0:T(8,128)(2,1)} %get-tuple-element.25.zi, bf16[256,64]{1,0:T(8,128)(2,1)} %dynamic-slice_bitcast_fusion.2.yi), custom_call_target="tpu_custom_call" | custom-call | tf_op jit(solution)/shard_map/input_gradient/pallas_call | solution.py:651
  151.6 0.0 copy-done.1
  151.6 0.7 slice_reduce_fusion
  152.3 0.0 copy-done
  152.3 0.7 copy.20
  153.0 0.6 copy.21
Async XLA Ops:
  138.3 13.3 %copy-start.1 = (f32[32,128]{1,0:T(8,128)S(1)}, f32[32,128]{1,0:T(8,128)}, u32[]{:S(2)}) copy-start(f32[32,128]{1,0:T(8,128)} %get-tuple-element.24) | copy-start | bytes 49156
  138.3 14.0 %copy-start = (f32[32,2048]{1,0:T(8,128)S(1)}, f32[32,2048]{1,0:T(8,128)}, u32[]{:S(2)}) copy-start(f32[32,2048]{1,0:T(8,128)} %get-tuple-element.34) | copy-start | bytes 786436

commit v2 on v0

v2 whole, which is shorter than its diff:
```python
import functools
import math

import jax
import jax.numpy as jnp
import numpy as np
from jax import lax
from jax.experimental import pallas as pl
from jax.experimental.pallas import tpu as pltpu

P = jax.sharding.PartitionSpec
BF = jnp.bfloat16
F32 = jnp.float32

C = 32
X = 2
Y = 2048
Z = 2048
K = 64
ROWS = 128
COLS = 256
G = 16
NG = ROWS // G

MESH = pl.DeviceIdType.MESH


def row_order():
    order = []
    for core in range(2):
        for cx in range(4):
            for cy in range(4):
                for lo in range(2):
                    order.append(cx * 16 + lo * 8 + core * 4 + cy)
    return np.array(order)


def make_tables():
    j = row_order()
    fy = np.where(j < K // 2, j, Y - K + j)
    y = np.arange(Y)
    ang_y = 2.0 * np.pi * ((fy[:, None] * y[None, :]) % Y) / Y
    z = np.arange(Z)
    ang_z = 2.0 * np.pi * ((np.arange(K)[:, None] * z[None, :]) % Z) / Z
    cy, sy = np.cos(ang_y), np.sin(ang_y)
    cz, sz = np.cos(ang_z), np.sin(ang_z)
    zf = np.concatenate([cz, -sz, -sz, -cz], axis=0)
    zf = zf.reshape(4 * K, Z // COLS, COLS).transpose(1, 0, 2)
    yf = np.stack([cy, sy], axis=0).reshape(2, K, Y // ROWS, ROWS)
    yf = yf.transpose(2, 1, 0, 3).reshape(Y // ROWS, K, 2 * ROWS)
    yi = np.stack([cy, sy], axis=0).reshape(2, K, Y // ROWS, ROWS)
    yi = yi.transpose(2, 0, 3, 1).reshape(Y // ROWS, 2 * ROWS, K)
    bf = lambda a: np.ascontiguousarray(a).astype(jnp.bfloat16)
    scale = 1.0 / math.sqrt(Y * Z)
    return (
        bf(zf.transpose(0, 2, 1)),
        bf(zf),
        bf(yf * scale),
        bf(yi * (2.0 * scale)),
    )


def make_spreads():
    lane = np.arange(C * C)
    rows = np.arange(C)[:, None]
    over_o = (lane[None, :] // C == rows).astype(np.float32)
    over_i = (lane[None, :] % C == rows).astype(np.float32)
    return over_o.astype(jnp.bfloat16), over_i.astype(jnp.bfloat16)


def dot(a, b):
    return jnp.dot(a, b, preferred_element_type=F32)


def dot_nt(a, b):
    return lax.dot_general(a, b, (((1,), (1,)), ((), ())), preferred_element_type=F32)


def split(v):
    hi = v.astype(BF)
    return hi, (v - hi.astype(F32)).astype(BF)


def forward_z(src, zf, rows):
    for c in range(0, C, 4):
        f = src[pl.ds(c, 4)].reshape(4 * ROWS, COLS)
        rows[pl.ds(c, 4)] = dot(f, zf[...]).astype(BF).reshape(4, ROWS, 4 * K)


def forward_y(rows, yf, wide, part):
    for c in range(0, C, 2):
        one, two = rows[c], rows[c + 1]
        upper = jnp.concatenate([one[:, : 2 * K], two[:, : 2 * K]], axis=1)
        lower = jnp.concatenate([one[:, 2 * K :], two[:, 2 * K :]], axis=1)
        r = dot(yf[...], jnp.concatenate([upper, lower], axis=0))
        wide[pl.ds(c, K, stride=C), :] = r[:, : 2 * K]
        wide[pl.ds(c + 1, K, stride=C), :] = r[:, 2 * K :]
    step = K * C // 8
    for n in range(8):
        part[n // 4, n % 4] = wide[pl.ds(n * step, step), :].astype(BF).reshape(4, 2, C, 2 * K)


def inverse_y(modes, yi, wide, spread):
    step = K * C // 8
    for n in range(8):
        wide[pl.ds(n * step, step), :] = modes[n // 4, n % 4].astype(F32).reshape(step, 2 * K)
    for c in range(0, C, 2):
        one = wide[pl.ds(c, K, stride=C), :].astype(BF)
        two = wide[pl.ds(c + 1, K, stride=C), :].astype(BF)
        r = dot(yi[...], jnp.concatenate([one, two], axis=1)).astype(BF)
        for e in range(2):
            lanes = slice(e * 2 * K, (e + 1) * 2 * K)
            spread[c + e, :, : 2 * K] = r[:ROWS, lanes]
            spread[c + e, :, 2 * K :] = r[ROWS:, lanes]


def rows_of(g):
    return pl.ds(g * G, G)


def places():
    gy, gz = lax.axis_index("gy"), lax.axis_index("gz")
    return dict(x=gy // 4, lo=gy // 2 % 2, core=gy % 2, y=gz // 2, hi=gz % 2)


def device(at, **other):
    at = dict(at, **other)
    return {
        "gy": at["x"] * 4 + at["lo"] * 2 + at["core"],
        "gz": at["y"] * 2 + at["hi"],
    }


def turned(at, axis, step):
    return lax.rem(at[axis] + step, 4)


STEPS = [(dx, dy, dl) for dx in (2, 1, 3, 0) for dy in (2, 1, 3, 0) for dl in (1, 0)][:-1]


def moved(at, step):
    dx, dy, dl = step
    lo = 1 - at["lo"] if dl else at["lo"]
    return dict(x=turned(at, "x", dx), y=turned(at, "y", dy), lo=lo)


def greet(at):
    barrier = pltpu.get_barrier_semaphore()
    partners = [device(at, core=1 - at["core"]), device(at, hi=1 - at["hi"])]
    partners += [device(at, **moved(at, step)) for step in STEPS]
    for partner in partners:
        pl.semaphore_signal(barrier, inc=1, device_id=partner, device_id_type=MESH)
    return barrier, len(partners)


def send(src, dst, sems, n, to):
    send_sem, recv_sem = sems
    copy = pltpu.make_async_remote_copy(
        src_ref=src,
        dst_ref=dst,
        send_sem=send_sem.at[n],
        recv_sem=recv_sem.at[n],
        device_id=to,
        device_id_type=MESH,
    )
    copy.start()
    return copy


def arrived(copies):
    for copy in copies:
        copy.wait()


def scatter_core(at, p, part, b):
    other = 1 - at["core"]
    return [send(part.at[p, other], b["r1"].at[p], b["core_in"], p, device(at, core=other))]


def scatter_rows(at, p, part, b):
    me = at["core"]
    for cx in range(4):
        b["s1"][p, cx] = (part[p, me, cx].astype(F32) + b["r1"][p, cx].astype(F32)).astype(BF)
    copies = []
    for n, step in enumerate(STEPS):
        to = moved(at, step)
        copies.append(
            send(
                b["s1"].at[p, to["x"], to["y"], to["lo"]],
                b["r2"].at[p, n],
                b["rows_in"],
                p * len(STEPS) + n,
                device(at, **to),
            )
        )
    return copies


def scatter_halves(at, p, b):
    total = b["s1"][p, at["x"], at["y"], at["lo"]].astype(F32)
    for n in range(len(STEPS)):
        total = total + b["r2"][p, n].astype(F32)
    b["s3"][p] = total
    return [send(b["s3"].at[p], b["r4"].at[p], b["half_in"], p, device(at, hi=1 - at["hi"]))]


def scatter_total(at, p, b):
    return b["s3"][p] + b["r4"][p]


def gather_rows(at, p, modes, b):
    here = modes.at[p, at["core"], at["x"], at["y"], at["lo"]]
    return [
        send(here, here, b["rows_out"], p * len(STEPS) + n, device(at, **moved(at, step)))
        for n, step in enumerate(STEPS)
    ]


def gather_core(at, p, modes, b, copies):
    passed = []
    for dx in (0, 1, 3, 2):
        arrived([copy for copy, step in zip(copies, STEPS) if step[0] == dx])
        block = modes.at[p, at["core"], turned(at, "x", 4 - dx)]
        passed.append(send(block, block, b["core_out"], 4 * p + dx, device(at, core=1 - at["core"])))
    return passed


def exchange_scratch():
    pair = lambda n: [pltpu.SemaphoreType.DMA((n,)), pltpu.SemaphoreType.DMA((n,))]
    rows = len(STEPS)
    return dict(
        r1=pltpu.VMEM((X, 4, 4, 2, C, 2 * K), BF),
        s1=pltpu.VMEM((X, 4, 4, 2, C, 2 * K), BF),
        r2=pltpu.VMEM((X, rows, C, 2 * K), BF),
        s3=pltpu.VMEM((X, C, 2 * K), F32),
        r4=pltpu.VMEM((X, C, 2 * K), F32),
        core_in=pair(X),
        rows_in=pair(X * rows),
        half_in=pair(X),
        rows_out=pair(X * rows),
        core_out=pair(4 * X),
    )


def widen(v, table):
    hi, lo = split(v)
    return dot(hi, table) + dot(lo, table)


def narrow(v, table):
    hi, lo = split(v)
    return dot_nt(hi, table) + dot_nt(lo, table)


def put_modes(at, p, modes, real, imag):
    block = jnp.concatenate([real, imag], axis=0).T
    modes[p, at["core"], at["x"], at["y"], at["lo"]] = block.astype(BF)


def mix(at, p, total, w_all, over_o, over_i, modes, spec):
    t = total.T
    spec[p] = t
    s_real = widen(t[:K], over_o)
    s_imag = widen(t[K:], over_o)
    w_real, w_imag = w_all[:, : C * C].astype(F32), w_all[:, C * C :].astype(F32)
    real = narrow(w_real * s_real - w_imag * s_imag, over_i)
    imag = narrow(w_real * s_imag + w_imag * s_real, over_i)
    put_modes(at, p, modes, real, imag)


def unmix(at, p, total, w_all, over_o, over_i, modes, dual):
    t = total.T * 2.0
    dual[p] = t
    d_real = widen(t[:K], over_i)
    d_imag = widen(t[K:], over_i)
    w_real, w_imag = w_all[:, : C * C].astype(F32), w_all[:, C * C :].astype(F32)
    real = narrow(w_real * d_real + w_imag * d_imag, over_o)
    imag = narrow(w_real * d_imag - w_imag * d_real, over_o)
    put_modes(at, p, modes, real * 0.5, imag * 0.5)


def weight_gradient(at, spec, dual, over_o, over_i, grad):
    half = K // 2
    real, imag = 0.0, 0.0
    for p in range(X):
        top = pl.ds(pl.multiple_of(at["hi"] * half, half), half)
        low = pl.ds(pl.multiple_of(at["hi"] * half + K, half), half)
        s_real, s_imag = widen(spec[p, top], over_o), widen(spec[p, low], over_o)
        d_real, d_imag = widen(dual[p, top], over_i), widen(dual[p, low], over_i)
        real = real + d_real * s_real + d_imag * s_imag
        imag = imag + d_imag * s_real - d_real * s_imag
    grad[:, : C * C] = real
    grad[:, C * C :] = imag


def gelu_terms(v):
    e = jnp.exp(v * v * -0.5)
    t = 1.0 / (1.0 + jnp.abs(v) * (0.3275911 / math.sqrt(2.0)))
    q = t * (0.5 * 1.061405429) - 0.5 * 1.453152027
    q = q * t + 0.5 * 1.421413741
    q = q * t - 0.5 * 0.284496736
    q = q * t + 0.5 * 0.254829592
    q = q * t * e
    phi = jnp.where(v >= 0.0, 1.0 - q, q)
    return v * phi, phi + v * e * (1.0 / math.sqrt(2.0 * math.pi))


def group_masks():
    a = lax.broadcasted_iota(jnp.int32, (C * G, C * G), 0)
    b = lax.broadcasted_iota(jnp.int32, (C * G, C * G), 1)
    same = lax.rem(a, G) == lax.rem(b, G)
    m = lax.broadcasted_iota(jnp.int32, (C * G, C), 0)
    n = lax.broadcasted_iota(jnp.int32, (C * G, C), 1)
    over = (m // G == n).astype(F32).astype(BF)
    return same, over


def kron_of(half, over, same):
    return jnp.where(same, dot_nt(half.astype(BF), over), 0.0).astype(BF)


def pointwise(f_buf, kron, bias_col, base):
    for g in range(NG):
        f = f_buf[:, rows_of(g), :].reshape(C * G, COLS)
        base[g] = dot(kron[...], f) + bias_col[:, :1]


def layer(spread, base, cot, zi, zf, o_buf, g_buf, rows, between=None):
    pre, slope_of = {}, {}
    for s in range(NG + 2):
        if s < NG:
            pre[s] = dot(spread[:, rows_of(s), :].reshape(C * G, 4 * K), zi[...]) + base[s]
        if 1 <= s <= NG:
            at = rows_of(s - 1)
            value, slope = gelu_terms(pre.pop(s - 1))
            o_buf[:, at, :] = value.astype(BF).reshape(C, G, COLS)
            gp = (cot[:, at, :].reshape(C * G, COLS).astype(F32) * slope).astype(BF)
            g_buf[:, at, :] = gp.reshape(C, G, COLS)
            slope_of[s - 1] = gp
        if s >= 2:
            r = dot(slope_of.pop(s - 2), zf[...]).astype(BF)
            rows[:, rows_of(s - 2), :] = r.reshape(C, G, 4 * K)
        if between is not None and s == NG // 2:
            between()


def point_gradient(g_buf, f_buf, acc, bias_acc, first):
    total, sums = 0.0, 0.0
    for q in range(0, NG, 4):
        gs = [g_buf[:, rows_of(q + e), :].reshape(C * G, COLS) for e in range(4)]
        fs = [f_buf[:, rows_of(q + e), :].reshape(C * G, COLS) for e in range(4)]
        total = total + dot_nt(jnp.concatenate(gs, axis=1), jnp.concatenate(fs, axis=1))
        for gp in gs:
            gp = gp.astype(F32)
            sums = sums + gp[:, : COLS // 2] + gp[:, COLS // 2 :]
    acc[...] = total if first else acc[...] + total
    bias_acc[...] = sums if first else bias_acc[...] + sums


def main_kernel(
    field, cot, weights, zf_all, zi_all, yf_all, yi_all, point, bias, over_o_ref, over_i_ref,
    out, gp_out, modes_out, grad, small_out,
    f_buf, c_buf, spread, rows, o_buf, g_buf, base, wide, part, modes, part2, modes2,
    zf, zi, yf, yi, kron, bias_col, acc, bias_acc, w_all, spec, dual, grad_buf, s_small, r_small,
    b1, b2, sems, w_sems, small_sems, out_sems,
):
    at = places()
    gy, gz = lax.axis_index("gy"), lax.axis_index("gz")
    local = pltpu.make_async_copy
    loads = [
        local(field.at[:, 0], f_buf.at[0], sems.at[0]),
        local(zf_all.at[gz], zf, sems.at[1]),
        local(yf_all.at[gy], yf, sems.at[2]),
        local(field.at[:, 1], f_buf.at[1], sems.at[3]),
        local(weights, w_all.at[at["hi"]], sems.at[4]),
        local(zi_all.at[gz], zi, sems.at[5]),
        local(yi_all.at[gy], yi, sems.at[6]),
        local(cot.at[:, 0], c_buf.at[0], sems.at[7]),
        local(cot.at[:, 1], c_buf.at[1], sems.at[8]),
    ]
    for load in loads[:4]:
        load.start()
    barrier, partners = greet(at)
    same, over = group_masks()
    kron[...] = kron_of(dot(over, point[...]), over, same)
    bias_wide = jnp.broadcast_to(bias[...].astype(F32), (2 * K, C)).astype(BF)
    bias_col[...] = dot_nt(over, bias_wide)
    over_o, over_i = over_o_ref[...], over_i_ref[...]

    for n in range(3):
        loads[n].wait()
    forward_z(f_buf.at[0], zf, rows.at[0])
    forward_y(rows.at[0], yf, wide.at[0], part.at[0])
    pl.semaphore_wait(barrier, partners)
    f0 = scatter_core(at, 0, part, b1)
    loads[3].wait()
    for load in loads[4:]:
        load.start()
    w_there = pltpu.make_async_remote_copy(
        src_ref=weights,
        dst_ref=w_all.at[at["hi"]],
        send_sem=w_sems.at[0],
        recv_sem=w_sems.at[1],
        device_id=device(at, hi=1 - at["hi"]),
        device_id_type=MESH,
    )
    forward_z(f_buf.at[1], zf, rows.at[1])
    arrived(f0)
    f0 = scatter_rows(at, 0, part, b1)
    forward_y(rows.at[1], yf, wide.at[1], part.at[1])
    f1 = scatter_core(at, 1, part, b1)
    w_there.start()
    pointwise(f_buf.at[0], kron, bias_col, base.at[0])
    arrived(f1)
    f1 = scatter_rows(at, 1, part, b1)
    pointwise(f_buf.at[1], kron, bias_col, base.at[1])
    arrived(f0)
    f0 = scatter_halves(at, 0, b1)
    arrived(f1)
    f1 = scatter_halves(at, 1, b1)
    for load in loads[4:]:
        load.wait()
    w_there.wait()
    w = w_all[...].reshape(K, 2 * C * C)
    arrived(f0)
    mix(at, 0, scatter_total(at, 0, b1), w, over_o, over_i, modes, spec)
    f0 = gather_rows(at, 0, modes, b1)
    arrived(f1)
    mix(at, 1, scatter_total(at, 1, b1), w, over_o, over_i, modes, spec)
    f1 = gather_rows(at, 1, modes, b1)
    f0 = gather_core(at, 0, modes, b1, f0)

    arrived(f0)
    inverse_y(modes.at[0], yi, wide.at[0], spread.at[0])
    f1 = gather_core(at, 1, modes, b1, f1)
    layer(spread.at[0], base.at[0], c_buf.at[0], zi, zf, o_buf.at[0], g_buf.at[0], rows.at[0])
    forward_y(rows.at[0], yf, wide.at[0], part2.at[0])
    f0 = scatter_core(at, 0, part2, b2)
    outs = [
        local(o_buf.at[0], out.at[:, 0], out_sems.at[0]),
        local(g_buf.at[0], gp_out.at[:, 0], out_sems.at[1]),
    ]
    outs[0].start()
    outs[1].start()
    arrived(f1)
    inverse_y(modes.at[1], yi, wide.at[1], spread.at[1])
    arrived(f0)
    f0 = scatter_rows(at, 0, part2, b2)
    layer(spread.at[1], base.at[1], c_buf.at[1], zi, zf, o_buf.at[1], g_buf.at[1], rows.at[1])
    forward_y(rows.at[1], yf, wide.at[1], part2.at[1])
    f1 = scatter_core(at, 1, part2, b2)
    outs += [
        local(o_buf.at[1], out.at[:, 1], out_sems.at[2]),
        local(g_buf.at[1], gp_out.at[:, 1], out_sems.at[3]),
    ]
    outs[2].start()
    outs[3].start()
    arrived(f0)
    f0 = scatter_halves(at, 0, b2)

    groups = [
        [device(at, core=1 - at["core"])],
        [device(at, x=turned(at, "x", s)) for s in (1, 2, 3)],
        [device(at, y=turned(at, "y", s)) for s in (1, 2, 3)],
        [device(at, lo=1 - at["lo"])],
        [device(at, hi=1 - at["hi"])],
    ]
    bases = (0, 1, 4, 7, 8)

    def small_send(n):
        return [
            send(s_small.at[n], r_small.at[bases[n] + e], small_sems, bases[n] + e, to)
            for e, to in enumerate(groups[n])
        ]

    def small_sum(n, copies):
        arrived(copies)
        total = s_small[n]
        for e in range(len(copies)):
            total = total + r_small[bases[n] + e]
        s_small[n + 1] = total

    arrived(f1)
    f1 = scatter_rows(at, 1, part2, b2)
    point_gradient(g_buf.at[0], f_buf.at[0], acc, bias_acc, True)
    arrived(f0)
    unmix(at, 0, scatter_total(at, 0, b2), w, over_o, over_i, modes2, dual)
    f0 = gather_rows(at, 0, modes2, b2)
    point_gradient(g_buf.at[1], f_buf.at[1], acc, bias_acc, False)
    arrived(f1)
    f1 = scatter_halves(at, 1, b2)
    kept = jnp.where(same, acc[...], 0.0).reshape(C, G, C * G).sum(axis=1)
    term = jnp.dot(kept, over.astype(F32), precision=lax.Precision.HIGHEST)
    total = bias_acc[...].reshape(C, G, COLS // 2).sum(axis=1).sum(axis=1, keepdims=True)
    s_small[0, :, :C] = term
    s_small[0, :, C:] = jnp.broadcast_to(total, (C, 2 * K - C))
    small = small_send(0)
    arrived(f1)
    unmix(at, 1, scatter_total(at, 1, b2), w, over_o, over_i, modes2, dual)
    f1 = gather_rows(at, 1, modes2, b2)
    small_sum(0, small)
    small = small_send(1)
    f0 = gather_core(at, 0, modes2, b2, f0)
    weight_gradient(at, spec, dual, over_o, over_i, grad_buf)
    outs.append(local(grad_buf, grad, out_sems.at[4]))
    outs[-1].start()
    small_sum(1, small)
    small = small_send(2)
    arrived(f0)
    outs.append(local(modes2.at[0], modes_out.at[0], out_sems.at[5]))
    outs[-1].start()
    small_sum(2, small)
    small = small_send(3)
    f1 = gather_core(at, 1, modes2, b2, f1)
    small_sum(3, small)
    small = small_send(4)
    arrived(f1)
    outs.append(local(modes2.at[1], modes_out.at[1], out_sems.at[6]))
    outs[-1].start()
    small_sum(4, small)
    small_out[...] = s_small[5] * (1.0 / math.sqrt(X * Y * Z))
    for copy in outs:
        copy.wait()


def last_kernel(
    held, gp, modes_in, zi_all, yi_all, grad_in, point, small,
    out, output, grad, term, total, modes, g_buf, h_buf, w_buf, spread, o_buf, wide, zi, yi, kron, sems, out_sems,
):
    gy, gz = lax.axis_index("gy"), lax.axis_index("gz")
    local = pltpu.make_async_copy
    loads = [
        local(modes_in.at[0], modes.at[0], sems.at[0]),
        local(yi_all.at[gy], yi, sems.at[1]),
        local(zi_all.at[gz], zi, sems.at[2]),
        local(gp.at[:, 0], g_buf.at[0], sems.at[3]),
        local(modes_in.at[1], modes.at[1], sems.at[4]),
        local(gp.at[:, 1], g_buf.at[1], sems.at[5]),
    ]
    passing = [local(held.at[:, x], h_buf.at[x], sems.at[6 + x]) for x in range(X)]
    passing.append(local(grad_in, w_buf, sems.at[8]))
    for load in loads + passing:
        load.start()
    term[...] = small[:, :C]
    total[...] = small[...].T[C : C + 1]
    same, over = group_masks()
    kron[...] = kron_of(dot_nt(over, point[...]), over, same)
    outs = []
    for x in range(X):
        for load in loads[:4] if x == 0 else loads[4:]:
            load.wait()
        inverse_y(modes.at[x], yi, wide.at[x], spread.at[x])
        for g in range(NG):
            at = rows_of(g)
            v = dot(spread[x, :, at, :].reshape(C * G, 4 * K), zi[...])
            v = v + dot(kron[...], g_buf[x, :, at, :].reshape(C * G, COLS))
            o_buf[x, :, at, :] = v.astype(BF).reshape(C, G, COLS)
        passing[x].wait()
        outs.append(local(h_buf.at[x], output.at[:, x], out_sems.at[2 + x]))
        outs[-1].start()
        outs.append(local(o_buf.at[x], out.at[:, x], out_sems.at[x]))
        outs[-1].start()
    passing[2].wait()
    outs.append(local(w_buf, grad, out_sems.at[4]))
    outs[-1].start()
    for copy in outs:
        copy.wait()


VMEM = pl.BlockSpec(memory_space=pltpu.VMEM)
ANY = pl.BlockSpec(memory_space=pl.ANY)
LIMIT = 60 * 1024 * 1024


def params(collective_id=None):
    if collective_id is None:
        return pltpu.CompilerParams(vmem_limit_bytes=LIMIT)
    return pltpu.CompilerParams(
        vmem_limit_bytes=LIMIT, collective_id=collective_id, has_side_effects=True
    )


def grid_buffer(dtype=BF):
    return pltpu.VMEM((X, C, ROWS, COLS), dtype)


def local(field, spec_weight, point_weight, bias, cotangent):
    zf, zi, yf, yi = (jnp.asarray(t) for t in make_tables())
    over_o, over_i = (jnp.asarray(t) for t in make_spreads())
    shape = jax.ShapeDtypeStruct
    deep = (X, 2, 4, 4, 2, C, 2 * K)
    lines = pltpu.VMEM((X, C, ROWS, 4 * K), BF)
    wide = pltpu.VMEM((X, K * C, 2 * K), F32)
    table = pltpu.VMEM((COLS, COLS), BF)
    vmem = pltpu.VMEM
    dma = pltpu.SemaphoreType.DMA
    square = (C * G, C * G)

    held, grad_pre, modes, grad_spec, small = pl.pallas_call(
        main_kernel,
        out_shape=(
            shape(field.shape, BF),
            shape(field.shape, BF),
            shape(deep, BF),
            shape((K // 2, 2 * C * C), F32),
            shape((C, 2 * K), F32),
        ),
        in_specs=[ANY] * 7 + [VMEM] * 4,
        out_specs=[ANY] * 4 + [VMEM],
        scratch_shapes=[
            grid_buffer(), grid_buffer(), lines, lines, grid_buffer(), grid_buffer(),
            vmem((X, NG, C * G, COLS), F32),
            wide, vmem(deep, BF), vmem(deep, BF), vmem(deep, BF), vmem(deep, BF),
            table, table, vmem((K, 2 * ROWS), BF), vmem((2 * ROWS, K), BF),
            vmem(square, BF), vmem((C * G, 2 * K), F32), vmem(square, F32),
            vmem((C * G, COLS // 2), F32),
            vmem((2, K // 2, 2 * C * C), BF),
            vmem((X, 2 * K, C), F32), vmem((X, 2 * K, C), F32),
            vmem((K // 2, 2 * C * C), F32),
            vmem((6, C, 2 * K), F32), vmem((9, C, 2 * K), F32),
            exchange_scratch(), exchange_scratch(),
            dma((9,)), dma((2,)), [dma((9,)), dma((9,))], dma((7,)),
        ],
        compiler_params=params(1),
        name="layer",
    )(
        field, cotangent, spec_weight, zf, zi, yf, yi,
        point_weight, bias.reshape(1, C), over_o, over_i,
    )

    grad_input, output, grad, term, total = pl.pallas_call(
        last_kernel,
        out_shape=(
            shape(field.shape, BF),
            shape(field.shape, BF),
            shape(grad_spec.shape, F32),
            shape((C, C), F32),
            shape((1, C), F32),
        ),
        in_specs=[ANY] * 6 + [VMEM] * 2,
        out_specs=[ANY] * 3 + [VMEM] * 2,
        scratch_shapes=[
            vmem(deep, BF), grid_buffer(), grid_buffer(), vmem(grad_spec.shape, F32),
            lines, grid_buffer(), wide,
            table, vmem((2 * ROWS, K), BF), vmem(square, BF), dma((9,)), dma((5,)),
        ],
        compiler_params=params(),
        name="input_gradient",
    )(held, grad_pre, modes, zi, yi, grad_spec, point_weight, small)

    return output, grad_input, grad, term, total.reshape(C)


def solution(mesh):
    grid = P(None, None, "gy", "gz")
    owned = P(("gy", "gz"), None)
    return jax.shard_map(
        local,
        mesh=mesh,
        in_specs=(grid, owned, P(), P(), grid),
        out_specs=(grid, grid, owned, P(), P()),
        check_vma=False,
    )
```

time: 2060 us -> 92.3 us (0.04)
  waiting for transfers between devices: 1780 us -> 0 us
  matrix products: 155 us -> 0 us
  Pallas kernels: 0 us -> 91.2 us
  blocking collectives: 62.8 us -> 0 us
  local copies, waits for them, and re-layouts: 37.7 us -> 0 us
    unnamed x6 -> x0, waiting for transfers between devices: 1280 us -> none
    all_gather x2 -> x0, waiting for transfers between devices: 491 us -> none  [to_grid(): lax.all_gather(modes.reshape(modes.shape[0], -1), ('gy', 'gz'), axis=0, t...]
    dot_general x35 -> x0, matrix products: 155 us -> none  [the longest x2 47.2 us: to_grid(): jnp.einsum('cxyq,qz->cxyz', spread, z_inverse_table(z_position), precisio...]
    pallas_call x0 -> x2, Pallas kernels: none -> 91.2 us  [the longest x1 80.2 us: local(): pl.pallas_call(main_kernel, out_shape=(shape(field.shape, BF), shape(fiel...]
    psum x1 -> x0, blocking collectives: 62.8 us -> none  [local(): point_total, bias_total = lax.psum((point_term, bias_term), ('gy', 'gz'))]
  transfers between devices with their start and end apart: 4 -> 0, of which waited for: 4 -> 0; matrix products, arithmetic and copies ran while one was open for 2% -> 0% of each run, Pallas kernels for 0% -> 0%
where the time goes in v2:
time: 92.3 us; the launch traced here: 92 us
  Pallas kernels  91.2 us (99%)
    pallas_call x1, Pallas kernels, local(): pl.pallas_call(main_kernel, out_shape=(shape(field.shape, BF), shape(fiel...  80.2 us
    pallas_call x1, Pallas kernels, local(): pl.pallas_call(last_kernel, out_shape=(shape(field.shape, BF), shape(fiel...  11 us

profile of v2, /device:TPU:0, one launch (start us, length us, event | category | flops | bytes accessed | tf_op | source)
XLA Modules:
  0.0 92.0 jit_solution(13829036910731984560)
XLA Ops:
  0.6 80.2 %layer.1 = (bf16[32,2,128,256]{3,2,1,0:T(8,128)(2,1)}, bf16[32,2,128,256]{3,2,1,0:T(8,128)(2,1)}, bf16[2,2,4,4,2,32,128]{6,5,4,3,2,1,0:T(8,128)(2,1)}, f32[32,2048]{1,0:T(8,128)}, f32[32,128]{1,0:T(8,128)}) custom-call(bf16[32,2,128,256]{3,2,1,0:T(8,128)(2,1)} %field.1, bf16[32,2,128,256]{3,2,1,0:T(8,128)(2,1)} %cot.1, bf16[32,2048]{1,0:T(8,128)(2,1)} %weights.1, ...), custom_call_target="tpu_custom_call" | custom-call | tf_op jit(solution)/shard_map/layer/pallas_call | solution.py:599
  80.9 11.0 %input_gradient.1 = (bf16[32,2,128,256]{3,2,1,0:T(8,128)(2,1)}, bf16[32,2,128,256]{3,2,1,0:T(8,128)(2,1)}, f32[32,2048]{1,0:T(8,128)}, f32[32,32]{1,0:T(8,128)}, f32[1,32]{1,0:T(1,128)}) custom-call(bf16[32,2,128,256]{3,2,1,0:T(8,128)(2,1)} %get-tuple-element.15.held, bf16[32,2,128,256]{3,2,1,0:T(8,128)(2,1)} %get-tuple-element.16.gp, ...), custom_call_target="tpu_custom_call" | custom-call | tf_op jit(solution)/shard_map/input_gradient/pallas_call | solution.py:631

commit v3 on v2

--- a/solution.py
+++ b/solution.py
@@ -81,8 +81,8 @@
     return hi, (v - hi.astype(F32)).astype(BF)
 
 
-def forward_z(src, zf, rows):
-    for c in range(0, C, 4):
+def forward_z(src, zf, rows, begin, end):
+    for c in range(begin, end, 4):
         f = src[pl.ds(c, 4)].reshape(4 * ROWS, COLS)
         rows[pl.ds(c, 4)] = dot(f, zf[...]).astype(BF).reshape(4, ROWS, 4 * K)
 
@@ -114,6 +114,14 @@
             spread[c + e, :, 2 * K :] = r[ROWS:, lanes]
 
 
+def fold(v):
+    return jnp.concatenate([v[8 * n : 8 * n + 8] for n in range(C // 8)], axis=1)
+
+
+def unfold(v):
+    return jnp.concatenate([v[:, C * n : C * n + C] for n in range(C // 8)], axis=0)
+
+
 def rows_of(g):
     return pl.ds(g * G, G)
 
@@ -144,10 +152,14 @@
     return dict(x=turned(at, "x", dx), y=turned(at, "y", dy), lo=lo)
 
 
+def across(at):
+    core, hi = 1 - at["core"], 1 - at["hi"]
+    return [device(at, core=core), device(at, hi=hi), device(at, core=core, hi=hi)]
+
+
 def greet(at):
     barrier = pltpu.get_barrier_semaphore()
-    partners = [device(at, core=1 - at["core"]), device(at, hi=1 - at["hi"])]
-    partners += [device(at, **moved(at, step)) for step in STEPS]
+    partners = across(at) + [device(at, **moved(at, step)) for step in STEPS]
     for partner in partners:
         pl.semaphore_signal(barrier, inc=1, device_id=partner, device_id_type=MESH)
     return barrier, len(partners)
@@ -325,6 +337,11 @@
         base[g] = dot(kron[...], f) + bias_col[:, :1]
 
 
+def pointwise_back(g_buf, kron, base):
+    for g in range(NG):
+        base[g] = dot(kron[...], g_buf[:, rows_of(g), :].reshape(C * G, COLS))
+
+
 def layer(spread, base, cot, zi, zf, o_buf, g_buf, rows, between=None):
     pre, slope_of = {}, {}
     for s in range(NG + 2):
@@ -359,43 +376,48 @@
 
 def main_kernel(
     field, cot, weights, zf_all, zi_all, yf_all, yi_all, point, bias, over_o_ref, over_i_ref,
-    out, gp_out, modes_out, grad, small_out,
-    f_buf, c_buf, spread, rows, o_buf, g_buf, base, wide, part, modes, part2, modes2,
-    zf, zi, yf, yi, kron, bias_col, acc, bias_acc, w_all, spec, dual, grad_buf, s_small, r_small,
-    b1, b2, sems, w_sems, small_sems, out_sems,
+    out, base, modes2, grad, zi, yi, small_out,
+    f_buf, c_buf, spread, rows, g_buf, wide, part, modes, part2,
+    zf, yf, kron, kron_back, bias_col, acc, bias_acc, w_all, spec, dual, s_small, r_small,
+    b1, b2, sems, w_sems, small_sems,
 ):
     at = places()
     gy, gz = lax.axis_index("gy"), lax.axis_index("gz")
     local = pltpu.make_async_copy
+    half = C // 2
     loads = [
-        local(field.at[:, 0], f_buf.at[0], sems.at[0]),
+        local(field.at[:half, 0], f_buf.at[0, :half], sems.at[0]),
         local(zf_all.at[gz], zf, sems.at[1]),
-        local(yf_all.at[gy], yf, sems.at[2]),
-        local(field.at[:, 1], f_buf.at[1], sems.at[3]),
-        local(weights, w_all.at[at["hi"]], sems.at[4]),
-        local(zi_all.at[gz], zi, sems.at[5]),
-        local(yi_all.at[gy], yi, sems.at[6]),
-        local(cot.at[:, 0], c_buf.at[0], sems.at[7]),
-        local(cot.at[:, 1], c_buf.at[1], sems.at[8]),
+        local(field.at[half:, 0], f_buf.at[0, half:], sems.at[2]),
+        local(yf_all.at[gy], yf, sems.at[3]),
+        local(field.at[:, 1], f_buf.at[1], sems.at[4]),
+        local(weights, w_all.at[at["hi"]], sems.at[5]),
+        local(zi_all.at[gz], zi, sems.at[6]),
+        local(yi_all.at[gy], yi, sems.at[7]),
+        local(cot.at[:, 0], c_buf.at[0], sems.at[8]),
+        local(cot.at[:, 1], c_buf.at[1], sems.at[9]),
     ]
-    for load in loads[:4]:
+    for load in loads[:5]:
         load.start()
     barrier, partners = greet(at)
-    same, over = group_masks()
-    kron[...] = kron_of(dot(over, point[...]), over, same)
-    bias_wide = jnp.broadcast_to(bias[...].astype(F32), (2 * K, C)).astype(BF)
-    bias_col[...] = dot_nt(over, bias_wide)
-    over_o, over_i = over_o_ref[...], over_i_ref[...]
-
-    for n in range(3):
-        loads[n].wait()
-    forward_z(f_buf.at[0], zf, rows.at[0])
+
+    loads[0].wait()
+    loads[1].wait()
+    forward_z(f_buf.at[0], zf, rows.at[0], 0, half)
+    loads[2].wait()
+    forward_z(f_buf.at[0], zf, rows.at[0], half, C)
+    loads[3].wait()
     forward_y(rows.at[0], yf, wide.at[0], part.at[0])
     pl.semaphore_wait(barrier, partners)
     f0 = scatter_core(at, 0, part, b1)
-    loads[3].wait()
-    for load in loads[4:]:
+    loads[4].wait()
+    for load in loads[5:]:
         load.start()
+    forward_z(f_buf.at[1], zf, rows.at[1], 0, C)
+    arrived(f0)
+    f0 = scatter_rows(at, 0, part, b1)
+    forward_y(rows.at[1], yf, wide.at[1], part.at[1])
+    f1 = scatter_core(at, 1, part, b1)
     w_there = pltpu.make_async_remote_copy(
         src_ref=weights,
         dst_ref=w_all.at[at["hi"]],
@@ -404,27 +426,28 @@
         device_id=device(at, hi=1 - at["hi"]),
         device_id_type=MESH,
     )
-    forward_z(f_buf.at[1], zf, rows.at[1])
-    arrived(f0)
-    f0 = scatter_rows(at, 0, part, b1)
-    forward_y(rows.at[1], yf, wide.at[1], part.at[1])
-    f1 = scatter_core(at, 1, part, b1)
     w_there.start()
-    pointwise(f_buf.at[0], kron, bias_col, base.at[0])
+    same, over = group_masks()
+    kron[...] = kron_of(dot(over, point[...]), over, same)
+    bias_wide = jnp.broadcast_to(bias[...].astype(F32), (2 * K, C)).astype(BF)
+    bias_col[...] = dot_nt(over, bias_wide)
+    over_o, over_i = over_o_ref[...], over_i_ref[...]
     arrived(f1)
     f1 = scatter_rows(at, 1, part, b1)
+    pointwise(f_buf.at[0], kron, bias_col, base.at[0])
+    arrived(f0)
+    f0 = scatter_halves(at, 0, b1)
     pointwise(f_buf.at[1], kron, bias_col, base.at[1])
-    arrived(f0)
-    f0 = scatter_halves(at, 0, b1)
-    arrived(f1)
-    f1 = scatter_halves(at, 1, b1)
-    for load in loads[4:]:
+    for load in loads[5:]:
         load.wait()
     w_there.wait()
     w = w_all[...].reshape(K, 2 * C * C)
     arrived(f0)
     mix(at, 0, scatter_total(at, 0, b1), w, over_o, over_i, modes, spec)
     f0 = gather_rows(at, 0, modes, b1)
+    arrived(f1)
+    f1 = scatter_halves(at, 1, b1)
+    kron_back[...] = kron_of(dot_nt(over, point[...]), over, same)
     arrived(f1)
     mix(at, 1, scatter_total(at, 1, b1), w, over_o, over_i, modes, spec)
     f1 = gather_rows(at, 1, modes, b1)
@@ -432,151 +455,96 @@
 
     arrived(f0)
     inverse_y(modes.at[0], yi, wide.at[0], spread.at[0])
-    f1 = gather_core(at, 1, modes, b1, f1)
-    layer(spread.at[0], base.at[0], c_buf.at[0], zi, zf, o_buf.at[0], g_buf.at[0], rows.at[0])
+    passed = []
+    layer(
+        spread.at[0], base.at[0], c_buf.at[0], zi, zf, out.at[0], g_buf.at[0], rows.at[0],
+        lambda: passed.extend(gather_core(at, 1, modes, b1, f1)),
+    )
     forward_y(rows.at[0], yf, wide.at[0], part2.at[0])
     f0 = scatter_core(at, 0, part2, b2)
-    outs = [
-        local(o_buf.at[0], out.at[:, 0], out_sems.at[0]),
-        local(g_buf.at[0], gp_out.at[:, 0], out_sems.at[1]),
-    ]
-    outs[0].start()
-    outs[1].start()
-    arrived(f1)
+    arrived(passed)
     inverse_y(modes.at[1], yi, wide.at[1], spread.at[1])
     arrived(f0)
     f0 = scatter_rows(at, 0, part2, b2)
-    layer(spread.at[1], base.at[1], c_buf.at[1], zi, zf, o_buf.at[1], g_buf.at[1], rows.at[1])
+    layer(spread.at[1], base.at[1], c_buf.at[1], zi, zf, out.at[1], g_buf.at[1], rows.at[1])
     forward_y(rows.at[1], yf, wide.at[1], part2.at[1])
     f1 = scatter_core(at, 1, part2, b2)
-    outs += [
-        local(o_buf.at[1], out.at[:, 1], out_sems.at[2]),
-        local(g_buf.at[1], gp_out.at[:, 1], out_sems.at[3]),
-    ]
-    outs[2].start()
-    outs[3].start()
     arrived(f0)
     f0 = scatter_halves(at, 0, b2)
-
-    groups = [
-        [device(at, core=1 - at["core"])],
-        [device(at, x=turned(at, "x", s)) for s in (1, 2, 3)],
-        [device(at, y=turned(at, "y", s)) for s in (1, 2, 3)],
-        [device(at, lo=1 - at["lo"])],
-        [device(at, hi=1 - at["hi"])],
-    ]
-    bases = (0, 1, 4, 7, 8)
-
-    def small_send(n):
-        return [
-            send(s_small.at[n], r_small.at[bases[n] + e], small_sems, bases[n] + e, to)
-            for e, to in enumerate(groups[n])
-        ]
-
-    def small_sum(n, copies):
-        arrived(copies)
-        total = s_small[n]
-        for e in range(len(copies)):
-            total = total + r_small[bases[n] + e]
-        s_small[n + 1] = total
-
     arrived(f1)
     f1 = scatter_rows(at, 1, part2, b2)
+
     point_gradient(g_buf.at[0], f_buf.at[0], acc, bias_acc, True)
     arrived(f0)
     unmix(at, 0, scatter_total(at, 0, b2), w, over_o, over_i, modes2, dual)
     f0 = gather_rows(at, 0, modes2, b2)
     point_gradient(g_buf.at[1], f_buf.at[1], acc, bias_acc, False)
-    arrived(f1)
-    f1 = scatter_halves(at, 1, b2)
     kept = jnp.where(same, acc[...], 0.0).reshape(C, G, C * G).sum(axis=1)
     term = jnp.dot(kept, over.astype(F32), precision=lax.Precision.HIGHEST)
     total = bias_acc[...].reshape(C, G, COLS // 2).sum(axis=1).sum(axis=1, keepdims=True)
-    s_small[0, :, :C] = term
-    s_small[0, :, C:] = jnp.broadcast_to(total, (C, 2 * K - C))
-    small = small_send(0)
+    s_small[0, :8] = fold(term)
+    s_small[0, 8:] = fold(jnp.broadcast_to(total, (C, C)))
+    arrived(f1)
+    f1 = scatter_halves(at, 1, b2)
+    small = [
+        send(s_small.at[0], r_small.at[n], small_sems, n, to) for n, to in enumerate(across(at))
+    ]
+    pointwise_back(g_buf.at[0], kron_back, base.at[0])
     arrived(f1)
     unmix(at, 1, scatter_total(at, 1, b2), w, over_o, over_i, modes2, dual)
     f1 = gather_rows(at, 1, modes2, b2)
-    small_sum(0, small)
-    small = small_send(1)
+    arrived(small)
+    s_small[1] = s_small[0] + r_small[0] + r_small[1] + r_small[2]
+    small = [
+        send(s_small.at[1], r_small.at[3 + n], small_sems, 3 + n, device(at, **moved(at, step)))
+        for n, step in enumerate(STEPS)
+    ]
     f0 = gather_core(at, 0, modes2, b2, f0)
-    weight_gradient(at, spec, dual, over_o, over_i, grad_buf)
-    outs.append(local(grad_buf, grad, out_sems.at[4]))
-    outs[-1].start()
-    small_sum(1, small)
-    small = small_send(2)
-    arrived(f0)
-    outs.append(local(modes2.at[0], modes_out.at[0], out_sems.at[5]))
-    outs[-1].start()
-    small_sum(2, small)
-    small = small_send(3)
+    weight_gradient(at, spec, dual, over_o, over_i, grad)
+    pointwise_back(g_buf.at[1], kron_back, base.at[1])
+    arrived(f0)
     f1 = gather_core(at, 1, modes2, b2, f1)
-    small_sum(3, small)
-    small = small_send(4)
+    arrived(small)
+    total = s_small[1]
+    for n in range(len(STEPS)):
+        total = total + r_small[3 + n]
+    small_out[...] = total * (1.0 / math.sqrt(X * Y * Z))
     arrived(f1)
-    outs.append(local(modes2.at[1], modes_out.at[1], out_sems.at[6]))
-    outs[-1].start()
-    small_sum(4, small)
-    small_out[...] = s_small[5] * (1.0 / math.sqrt(X * Y * Z))
+
+
+def last_kernel(
+    held, base, modes, grad_in, zi, yi, small,
+    out, output, grad, term, total, spread, o_buf, wide, out_sems,
+):
+    local = pltpu.make_async_copy
+    outs = [local(held.at[x], output.at[:, x], out_sems.at[x]) for x in range(X)]
+    outs.append(local(grad_in, grad, out_sems.at[2]))
     for copy in outs:
-        copy.wait()
-
-
-def last_kernel(
-    held, gp, modes_in, zi_all, yi_all, grad_in, point, small,
-    out, output, grad, term, total, modes, g_buf, h_buf, w_buf, spread, o_buf, wide, zi, yi, kron, sems, out_sems,
-):
-    gy, gz = lax.axis_index("gy"), lax.axis_index("gz")
-    local = pltpu.make_async_copy
-    loads = [
-        local(modes_in.at[0], modes.at[0], sems.at[0]),
-        local(yi_all.at[gy], yi, sems.at[1]),
-        local(zi_all.at[gz], zi, sems.at[2]),
-        local(gp.at[:, 0], g_buf.at[0], sems.at[3]),
-        local(modes_in.at[1], modes.at[1], sems.at[4]),
-        local(gp.at[:, 1], g_buf.at[1], sems.at[5]),
-    ]
-    passing = [local(held.at[:, x], h_buf.at[x], sems.at[6 + x]) for x in range(X)]
-    passing.append(local(grad_in, w_buf, sems.at[8]))
-    for load in loads + passing:
-        load.start()
-    term[...] = small[:, :C]
-    total[...] = small[...].T[C : C + 1]
-    same, over = group_masks()
-    kron[...] = kron_of(dot_nt(over, point[...]), over, same)
-    outs = []
+        copy.start()
+    term[...] = unfold(small[:8])
+    total[...] = unfold(small[8:]).T[:1]
     for x in range(X):
-        for load in loads[:4] if x == 0 else loads[4:]:
-            load.wait()
         inverse_y(modes.at[x], yi, wide.at[x], spread.at[x])
         for g in range(NG):
             at = rows_of(g)
-            v = dot(spread[x, :, at, :].reshape(C * G, 4 * K), zi[...])
-            v = v + dot(kron[...], g_buf[x, :, at, :].reshape(C * G, COLS))
+            v = dot(spread[x, :, at, :].reshape(C * G, 4 * K), zi[...]) + base[x, g]
             o_buf[x, :, at, :] = v.astype(BF).reshape(C, G, COLS)
-        passing[x].wait()
-        outs.append(local(h_buf.at[x], output.at[:, x], out_sems.at[2 + x]))
+        outs.append(local(o_buf.at[x], out.at[:, x], out_sems.at[3 + x]))
         outs[-1].start()
-        outs.append(local(o_buf.at[x], out.at[:, x], out_sems.at[x]))
-        outs[-1].start()
-    passing[2].wait()
-    outs.append(local(w_buf, grad, out_sems.at[4]))
-    outs[-1].start()
     for copy in outs:
         copy.wait()
 
 
 VMEM = pl.BlockSpec(memory_space=pltpu.VMEM)
 ANY = pl.BlockSpec(memory_space=pl.ANY)
-LIMIT = 60 * 1024 * 1024
-
-
-def params(collective_id=None):
+
+
+def params(mib, collective_id=None):
+    limit = mib * 1024 * 1024
     if collective_id is None:
-        return pltpu.CompilerParams(vmem_limit_bytes=LIMIT)
+        return pltpu.CompilerParams(vmem_limit_bytes=limit)
     return pltpu.CompilerParams(
-        vmem_limit_bytes=LIMIT, collective_id=collective_id, has_side_effects=True
+        vmem_limit_bytes=limit, collective_id=collective_id, has_side_effects=True
     )
 
 
@@ -596,32 +564,32 @@
     dma = pltpu.SemaphoreType.DMA
     square = (C * G, C * G)
 
-    held, grad_pre, modes, grad_spec, small = pl.pallas_call(
+    held, base, modes, grad_spec, zi, yi, small = pl.pallas_call(
         main_kernel,
         out_shape=(
-            shape(field.shape, BF),
-            shape(field.shape, BF),
-            shape(deep, BF),
-            shape((K // 2, 2 * C * C), F32),
-            shape((C, 2 * K), F32),
+            grid_buffer(),
+            vmem((X, NG, C * G, COLS), F32),
+            vmem(deep, BF),
+            vmem((K // 2, 2 * C * C), F32),
+            table,
+            vmem((2 * ROWS, K), BF),
+            vmem((16, 4 * C), F32),
         ),
         in_specs=[ANY] * 7 + [VMEM] * 4,
-        out_specs=[ANY] * 4 + [VMEM],
+        out_specs=[VMEM] * 7,
         scratch_shapes=[
-            grid_buffer(), grid_buffer(), lines, lines, grid_buffer(), grid_buffer(),
-            vmem((X, NG, C * G, COLS), F32),
-            wide, vmem(deep, BF), vmem(deep, BF), vmem(deep, BF), vmem(deep, BF),
-            table, table, vmem((K, 2 * ROWS), BF), vmem((2 * ROWS, K), BF),
-            vmem(square, BF), vmem((C * G, 2 * K), F32), vmem(square, F32),
+            grid_buffer(), grid_buffer(), lines, lines, grid_buffer(),
+            wide, vmem(deep, BF), vmem(deep, BF), vmem(deep, BF),
+            table, vmem((K, 2 * ROWS), BF),
+            vmem(square, BF), vmem(square, BF), vmem((C * G, 2 * K), F32), vmem(square, F32),
             vmem((C * G, COLS // 2), F32),
             vmem((2, K // 2, 2 * C * C), BF),
             vmem((X, 2 * K, C), F32), vmem((X, 2 * K, C), F32),
-            vmem((K // 2, 2 * C * C), F32),
-            vmem((6, C, 2 * K), F32), vmem((9, C, 2 * K), F32),
+            vmem((2, 16, 4 * C), F32), vmem((3 + len(STEPS), 16, 4 * C), F32),
             exchange_scratch(), exchange_scratch(),
-            dma((9,)), dma((2,)), [dma((9,)), dma((9,))], dma((7,)),
+            dma((10,)), dma((2,)), [dma((3 + len(STEPS),)), dma((3 + len(STEPS),))],
         ],
-        compiler_params=params(1),
+        compiler_params=params(46, 1),
         name="layer",
     )(
         field, cotangent, spec_weight, zf, zi, yf, yi,
@@ -637,16 +605,12 @@
             shape((C, C), F32),
             shape((1, C), F32),
         ),
-        in_specs=[ANY] * 6 + [VMEM] * 2,
+        in_specs=[VMEM] * 7,
         out_specs=[ANY] * 3 + [VMEM] * 2,
-        scratch_shapes=[
-            vmem(deep, BF), grid_buffer(), grid_buffer(), vmem(grad_spec.shape, F32),
-            lines, grid_buffer(), wide,
-            table, vmem((2 * ROWS, K), BF), vmem(square, BF), dma((9,)), dma((5,)),
-        ],
-        compiler_params=params(),
+        scratch_shapes=[lines, grid_buffer(), wide, dma((5,))],
+        compiler_params=params(24),
         name="input_gradient",
-    )(held, grad_pre, modes, zi, yi, grad_spec, point_weight, small)
+    )(held, base, modes, grad_spec, zi, yi, small)
 
     return output, grad_input, grad, term, total.reshape(C)
 

time: 92.3 us -> 78.9 us (0.85)
  Pallas kernels: 91.2 us -> 77.3 us
    pallas_call x1, Pallas kernels: 80.2 us -> 72 us  [local(): pl.pallas_call(main_kernel, out_shape=(grid_buffer(), vmem((X, NG, C * G,...]
    pallas_call x1, Pallas kernels: 11 us -> 5.35 us  [local(): pl.pallas_call(last_kernel, out_shape=(shape(field.shape, BF), shape(fiel...]
where the time goes in v3:
time: 78.9 us; the launch traced here: 78.2 us
  Pallas kernels  77.3 us (98%)
  between operations  0.82 us (1%)
    pallas_call x1, Pallas kernels, local(): pl.pallas_call(main_kernel, out_shape=(grid_buffer(), vmem((X, NG, C * G,...  72 us
    pallas_call x1, Pallas kernels, local(): pl.pallas_call(last_kernel, out_shape=(shape(field.shape, BF), shape(fiel...  5.35 us

profile of v3, /device:TPU:0, one launch (start us, length us, event | category | flops | bytes accessed | tf_op | source)
XLA Modules:
  0.0 78.2 jit_solution(9047067568155733287)
XLA Ops:
  0.6 72.0 %layer.1 = (bf16[2,32,128,256]{3,2,1,0:T(8,128)(2,1)S(1)}, f32[2,8,512,256]{3,2,1,0:T(8,128)S(1)}, bf16[2,2,4,4,2,32,128]{6,5,4,3,2,1,0:T(8,128)(2,1)S(1)}, f32[...) custom-call(bf16[32,2,128,256]{3,2,1,0:T(8,128)(2,1)} %field.1, ...), custom_call_target="tpu_custom_call" | custom-call | tf_op jit(solution)/shard_map/layer/pallas_call | solution.py:567
  72.6 5.3 %input_gradient.1 = (bf16[32,2,128,256]{3,2,1,0:T(8,128)(2,1)}, bf16[32,2,128,256]{3,2,1,0:T(8,128)(2,1)}, f32[32,2048]{1,0:T(8,128)}, f32[32,32]{1,0:T(8,128)}, f32[1,32]{1,0:T(1,128)}) custom-call(bf16[2,32,128,256]{3,2,1,0:T(8,128)(2,1)S(1)} %get-tuple-element.17.held, f32[2,8,512,256]{3,2,1,0:T(8,128)S(1)} %get-tuple-element.18.base, ...), custom_call_target="tpu_custom_call" | custom-call | tf_op jit(solution)/shard_map/input_gradient/pallas_call | solution.py:599

commit v4 on v3

--- a/solution.py
+++ b/solution.py
@@ -306,24 +306,18 @@
 
 
 def gelu_terms(v):
-    e = jnp.exp(v * v * -0.5)
-    t = 1.0 / (1.0 + jnp.abs(v) * (0.3275911 / math.sqrt(2.0)))
-    q = t * (0.5 * 1.061405429) - 0.5 * 1.453152027
-    q = q * t + 0.5 * 1.421413741
-    q = q * t - 0.5 * 0.284496736
-    q = q * t + 0.5 * 0.254829592
-    q = q * t * e
-    phi = jnp.where(v >= 0.0, 1.0 - q, q)
-    return v * phi, phi + v * e * (1.0 / math.sqrt(2.0 * math.pi))
+    phi = 0.5 + 0.5 * lax.erf(v * math.sqrt(0.5))
+    return v * phi, phi + v * jnp.exp(v * v * -0.5) * (1.0 / math.sqrt(2.0 * math.pi))
 
 
 def group_masks():
     a = lax.broadcasted_iota(jnp.int32, (C * G, C * G), 0)
     b = lax.broadcasted_iota(jnp.int32, (C * G, C * G), 1)
-    same = lax.rem(a, G) == lax.rem(b, G)
+    same = ((a ^ b) & (G - 1)) == 0
     m = lax.broadcasted_iota(jnp.int32, (C * G, C), 0)
     n = lax.broadcasted_iota(jnp.int32, (C * G, C), 1)
-    over = (m // G == n).astype(F32).astype(BF)
+    over = (m - n * G).astype(F32)
+    over = jnp.where((over >= 0.0) & (over < float(G)), 1.0, 0.0).astype(BF)
     return same, over
 
 
@@ -342,7 +336,7 @@
         base[g] = dot(kron[...], g_buf[:, rows_of(g), :].reshape(C * G, COLS))
 
 
-def layer(spread, base, cot, zi, zf, o_buf, g_buf, rows, between=None):
+def layer(spread, base, cot, zi, zf, o_buf, g_buf, rows):
     pre, slope_of = {}, {}
     for s in range(NG + 2):
         if s < NG:
@@ -357,8 +351,6 @@
         if s >= 2:
             r = dot(slope_of.pop(s - 2), zf[...]).astype(BF)
             rows[:, rows_of(s - 2), :] = r.reshape(C, G, 4 * K)
-        if between is not None and s == NG // 2:
-            between()
 
 
 def point_gradient(g_buf, f_buf, acc, bias_acc, first):
@@ -410,14 +402,6 @@
     forward_y(rows.at[0], yf, wide.at[0], part.at[0])
     pl.semaphore_wait(barrier, partners)
     f0 = scatter_core(at, 0, part, b1)
-    loads[4].wait()
-    for load in loads[5:]:
-        load.start()
-    forward_z(f_buf.at[1], zf, rows.at[1], 0, C)
-    arrived(f0)
-    f0 = scatter_rows(at, 0, part, b1)
-    forward_y(rows.at[1], yf, wide.at[1], part.at[1])
-    f1 = scatter_core(at, 1, part, b1)
     w_there = pltpu.make_async_remote_copy(
         src_ref=weights,
         dst_ref=w_all.at[at["hi"]],
@@ -427,6 +411,12 @@
         device_id_type=MESH,
     )
     w_there.start()
+    loads[4].wait()
+    forward_z(f_buf.at[1], zf, rows.at[1], 0, C)
+    arrived(f0)
+    f0 = scatter_rows(at, 0, part, b1)
+    forward_y(rows.at[1], yf, wide.at[1], part.at[1])
+    f1 = scatter_core(at, 1, part, b1)
     same, over = group_masks()
     kron[...] = kron_of(dot(over, point[...]), over, same)
     bias_wide = jnp.broadcast_to(bias[...].astype(F32), (2 * K, C)).astype(BF)
@@ -434,6 +424,8 @@
     over_o, over_i = over_o_ref[...], over_i_ref[...]
     arrived(f1)
     f1 = scatter_rows(at, 1, part, b1)
+    for load in loads[5:]:
+        load.start()
     pointwise(f_buf.at[0], kron, bias_col, base.at[0])
     arrived(f0)
     f0 = scatter_halves(at, 0, b1)
@@ -455,46 +447,44 @@
 
     arrived(f0)
     inverse_y(modes.at[0], yi, wide.at[0], spread.at[0])
-    passed = []
-    layer(
-        spread.at[0], base.at[0], c_buf.at[0], zi, zf, out.at[0], g_buf.at[0], rows.at[0],
-        lambda: passed.extend(gather_core(at, 1, modes, b1, f1)),
-    )
+    layer(spread.at[0], base.at[0], c_buf.at[0], zi, zf, out.at[0], g_buf.at[0], rows.at[0])
+    f1 = gather_core(at, 1, modes, b1, f1)
     forward_y(rows.at[0], yf, wide.at[0], part2.at[0])
     f0 = scatter_core(at, 0, part2, b2)
-    arrived(passed)
+    arrived(f1)
     inverse_y(modes.at[1], yi, wide.at[1], spread.at[1])
     arrived(f0)
     f0 = scatter_rows(at, 0, part2, b2)
     layer(spread.at[1], base.at[1], c_buf.at[1], zi, zf, out.at[1], g_buf.at[1], rows.at[1])
     forward_y(rows.at[1], yf, wide.at[1], part2.at[1])
     f1 = scatter_core(at, 1, part2, b2)
+
+    point_gradient(g_buf.at[0], f_buf.at[0], acc, bias_acc, True)
+    arrived(f1)
+    f1 = scatter_rows(at, 1, part2, b2)
     arrived(f0)
     f0 = scatter_halves(at, 0, b2)
-    arrived(f1)
-    f1 = scatter_rows(at, 1, part2, b2)
-
-    point_gradient(g_buf.at[0], f_buf.at[0], acc, bias_acc, True)
-    arrived(f0)
-    unmix(at, 0, scatter_total(at, 0, b2), w, over_o, over_i, modes2, dual)
-    f0 = gather_rows(at, 0, modes2, b2)
     point_gradient(g_buf.at[1], f_buf.at[1], acc, bias_acc, False)
+    same, over = group_masks()
     kept = jnp.where(same, acc[...], 0.0).reshape(C, G, C * G).sum(axis=1)
     term = jnp.dot(kept, over.astype(F32), precision=lax.Precision.HIGHEST)
     total = bias_acc[...].reshape(C, G, COLS // 2).sum(axis=1).sum(axis=1, keepdims=True)
     s_small[0, :8] = fold(term)
     s_small[0, 8:] = fold(jnp.broadcast_to(total, (C, C)))
-    arrived(f1)
-    f1 = scatter_halves(at, 1, b2)
     small = [
         send(s_small.at[0], r_small.at[n], small_sems, n, to) for n, to in enumerate(across(at))
     ]
+    arrived(f0)
+    unmix(at, 0, scatter_total(at, 0, b2), w, over_o, over_i, modes2, dual)
+    f0 = gather_rows(at, 0, modes2, b2)
+    arrived(f1)
+    f1 = scatter_halves(at, 1, b2)
     pointwise_back(g_buf.at[0], kron_back, base.at[0])
+    arrived(small)
+    s_small[1] = s_small[0] + r_small[0] + r_small[1] + r_small[2]
     arrived(f1)
     unmix(at, 1, scatter_total(at, 1, b2), w, over_o, over_i, modes2, dual)
     f1 = gather_rows(at, 1, modes2, b2)
-    arrived(small)
-    s_small[1] = s_small[0] + r_small[0] + r_small[1] + r_small[2]
     small = [
         send(s_small.at[1], r_small.at[3 + n], small_sems, 3 + n, device(at, **moved(at, step)))
         for n, step in enumerate(STEPS)

time: 78.9 us -> 74.9 us (0.949)
  Pallas kernels: 77.3 us -> 73.2 us
    pallas_call x1, Pallas kernels: 72 us -> 67.9 us  [local(): pl.pallas_call(main_kernel, out_shape=(grid_buffer(), vmem((X, NG, C * G,...]
where the time goes in v4:
time: 74.9 us; the launch traced here: 74.1 us
  Pallas kernels  73.2 us (98%)
  between operations  0.82 us (1%)
    pallas_call x1, Pallas kernels, local(): pl.pallas_call(main_kernel, out_shape=(grid_buffer(), vmem((X, NG, C * G,...  67.9 us
    pallas_call x1, Pallas kernels, local(): pl.pallas_call(last_kernel, out_shape=(shape(field.shape, BF), shape(fiel...  5.35 us

profile of v4, /device:TPU:0, one launch (start us, length us, event | category | flops | bytes accessed | tf_op | source)
XLA Modules:
  0.0 74.1 jit_solution(11677895526057668004)
XLA Ops:
  0.6 67.9 %layer.1 = (bf16[2,32,128,256]{3,2,1,0:T(8,128)(2,1)S(1)}, f32[2,8,512,256]{3,2,1,0:T(8,128)S(1)}, bf16[2,2,4,4,2,32,128]{6,5,4,3,2,1,0:T(8,128)(2,1)S(1)}, f32[...) custom-call(bf16[32,2,128,256]{3,2,1,0:T(8,128)(2,1)} %field.1, ...), custom_call_target="tpu_custom_call" | custom-call | tf_op jit(solution)/shard_map/layer/pallas_call | solution.py:557
  68.5 5.3 %input_gradient.1 = (bf16[32,2,128,256]{3,2,1,0:T(8,128)(2,1)}, bf16[32,2,128,256]{3,2,1,0:T(8,128)(2,1)}, f32[32,2048]{1,0:T(8,128)}, f32[32,32]{1,0:T(8,128)}, f32[1,32]{1,0:T(1,128)}) custom-call(bf16[2,32,128,256]{3,2,1,0:T(8,128)(2,1)S(1)} %get-tuple-element.17.held, f32[2,8,512,256]{3,2,1,0:T(8,128)S(1)} %get-tuple-element.18.base, ...), custom_call_target="tpu_custom_call" | custom-call | tf_op jit(solution)/shard_map/input_gradient/pallas_call | solution.py:589

commit v5 on v4

--- a/solution.py
+++ b/solution.py
@@ -191,20 +191,22 @@
 
 def scatter_rows(at, p, part, b):
     me = at["core"]
-    for cx in range(4):
+    copies = []
+    for dx in (2, 1, 3, 0):
+        cx = turned(at, "x", dx)
         b["s1"][p, cx] = (part[p, me, cx].astype(F32) + b["r1"][p, cx].astype(F32)).astype(BF)
-    copies = []
-    for n, step in enumerate(STEPS):
-        to = moved(at, step)
-        copies.append(
-            send(
-                b["s1"].at[p, to["x"], to["y"], to["lo"]],
-                b["r2"].at[p, n],
-                b["rows_in"],
-                p * len(STEPS) + n,
-                device(at, **to),
-            )
-        )
+        for n, step in enumerate(STEPS):
+            if step[0] == dx:
+                to = moved(at, step)
+                copies.append(
+                    send(
+                        b["s1"].at[p, cx, to["y"], to["lo"]],
+                        b["r2"].at[p, n],
+                        b["rows_in"],
+                        p * len(STEPS) + n,
+                        device(at, **to),
+                    )
+                )
     return copies
 
 
@@ -353,6 +355,14 @@
             rows[:, rows_of(s - 2), :] = r.reshape(C, G, 4 * K)
 
 
+def input_gradient(modes, base, zi, yi, wide, spread, out):
+    inverse_y(modes, yi, wide, spread)
+    for g in range(NG):
+        at = rows_of(g)
+        v = dot(spread[:, at, :].reshape(C * G, 4 * K), zi[...]) + base[g]
+        out[:, at, :] = v.astype(BF).reshape(C, G, COLS)
+
+
 def point_gradient(g_buf, f_buf, acc, bias_acc, first):
     total, sums = 0.0, 0.0
     for q in range(0, NG, 4):
@@ -368,8 +378,8 @@
 
 def main_kernel(
     field, cot, weights, zf_all, zi_all, yf_all, yi_all, point, bias, over_o_ref, over_i_ref,
-    out, base, modes2, grad, zi, yi, small_out,
-    f_buf, c_buf, spread, rows, g_buf, wide, part, modes, part2,
+    out, first, base1, modes_out, grad, zi, yi, small_out,
+    f_buf, c_buf, spread, rows, g_buf, base0, wide, part, modes, part2, modes2,
     zf, yf, kron, kron_back, bias_col, acc, bias_acc, w_all, spec, dual, s_small, r_small,
     b1, b2, sems, w_sems, small_sems,
 ):
@@ -389,9 +399,9 @@
         local(cot.at[:, 0], c_buf.at[0], sems.at[8]),
         local(cot.at[:, 1], c_buf.at[1], sems.at[9]),
     ]
+    barrier, partners = greet(at)
     for load in loads[:5]:
         load.start()
-    barrier, partners = greet(at)
 
     loads[0].wait()
     loads[1].wait()
@@ -410,7 +420,6 @@
         device_id=device(at, hi=1 - at["hi"]),
         device_id_type=MESH,
     )
-    w_there.start()
     loads[4].wait()
     forward_z(f_buf.at[1], zf, rows.at[1], 0, C)
     arrived(f0)
@@ -424,13 +433,16 @@
     over_o, over_i = over_o_ref[...], over_i_ref[...]
     arrived(f1)
     f1 = scatter_rows(at, 1, part, b1)
-    for load in loads[5:]:
+    w_there.start()
+    for load in loads[5:8]:
         load.start()
-    pointwise(f_buf.at[0], kron, bias_col, base.at[0])
+    pointwise(f_buf.at[0], kron, bias_col, base0)
     arrived(f0)
     f0 = scatter_halves(at, 0, b1)
-    pointwise(f_buf.at[1], kron, bias_col, base.at[1])
-    for load in loads[5:]:
+    for load in loads[8:]:
+        load.start()
+    pointwise(f_buf.at[1], kron, bias_col, base1)
+    for load in loads[5:8]:
         load.wait()
     w_there.wait()
     w = w_all[...].reshape(K, 2 * C * C)
@@ -445,9 +457,11 @@
     f1 = gather_rows(at, 1, modes, b1)
     f0 = gather_core(at, 0, modes, b1, f0)
 
+    for load in loads[8:]:
+        load.wait()
     arrived(f0)
     inverse_y(modes.at[0], yi, wide.at[0], spread.at[0])
-    layer(spread.at[0], base.at[0], c_buf.at[0], zi, zf, out.at[0], g_buf.at[0], rows.at[0])
+    layer(spread.at[0], base0, c_buf.at[0], zi, zf, out.at[0], g_buf.at[0], rows.at[0])
     f1 = gather_core(at, 1, modes, b1, f1)
     forward_y(rows.at[0], yf, wide.at[0], part2.at[0])
     f0 = scatter_core(at, 0, part2, b2)
@@ -455,7 +469,7 @@
     inverse_y(modes.at[1], yi, wide.at[1], spread.at[1])
     arrived(f0)
     f0 = scatter_rows(at, 0, part2, b2)
-    layer(spread.at[1], base.at[1], c_buf.at[1], zi, zf, out.at[1], g_buf.at[1], rows.at[1])
+    layer(spread.at[1], base1, c_buf.at[1], zi, zf, out.at[1], g_buf.at[1], rows.at[1])
     forward_y(rows.at[1], yf, wide.at[1], part2.at[1])
     f1 = scatter_core(at, 1, part2, b2)
 
@@ -479,7 +493,8 @@
     f0 = gather_rows(at, 0, modes2, b2)
     arrived(f1)
     f1 = scatter_halves(at, 1, b2)
-    pointwise_back(g_buf.at[0], kron_back, base.at[0])
+    pointwise_back(g_buf.at[0], kron_back, base0)
+    pointwise_back(g_buf.at[1], kron_back, base1)
     arrived(small)
     s_small[1] = s_small[0] + r_small[0] + r_small[1] + r_small[2]
     arrived(f1)
@@ -489,10 +504,10 @@
         send(s_small.at[1], r_small.at[3 + n], small_sems, 3 + n, device(at, **moved(at, step)))
         for n, step in enumerate(STEPS)
     ]
+    weight_gradient(at, spec, dual, over_o, over_i, grad)
     f0 = gather_core(at, 0, modes2, b2, f0)
-    weight_gradient(at, spec, dual, over_o, over_i, grad)
-    pointwise_back(g_buf.at[1], kron_back, base.at[1])
-    arrived(f0)
+    arrived(f0)
+    input_gradient(modes2.at[0], base0, zi, yi, wide.at[0], spread.at[0], first)
     f1 = gather_core(at, 1, modes2, b2, f1)
     arrived(small)
     total = s_small[1]
@@ -500,27 +515,27 @@
         total = total + r_small[3 + n]
     small_out[...] = total * (1.0 / math.sqrt(X * Y * Z))
     arrived(f1)
+    modes_out[...] = modes2[1]
 
 
 def last_kernel(
-    held, base, modes, grad_in, zi, yi, small,
-    out, output, grad, term, total, spread, o_buf, wide, out_sems,
+    held, first, base, modes, grad_in, zi, yi, small,
+    out, output, grad, term, total, spread, second, wide, out_sems,
 ):
     local = pltpu.make_async_copy
-    outs = [local(held.at[x], output.at[:, x], out_sems.at[x]) for x in range(X)]
-    outs.append(local(grad_in, grad, out_sems.at[2]))
+    outs = [
+        local(first, out.at[:, 0], out_sems.at[0]),
+        local(held.at[0], output.at[:, 0], out_sems.at[1]),
+        local(held.at[1], output.at[:, 1], out_sems.at[2]),
+        local(grad_in, grad, out_sems.at[3]),
+    ]
     for copy in outs:
         copy.start()
     term[...] = unfold(small[:8])
     total[...] = unfold(small[8:]).T[:1]
-    for x in range(X):
-        inverse_y(modes.at[x], yi, wide.at[x], spread.at[x])
-        for g in range(NG):
-            at = rows_of(g)
-            v = dot(spread[x, :, at, :].reshape(C * G, 4 * K), zi[...]) + base[x, g]
-            o_buf[x, :, at, :] = v.astype(BF).reshape(C, G, COLS)
-        outs.append(local(o_buf.at[x], out.at[:, x], out_sems.at[3 + x]))
-        outs[-1].start()
+    input_gradient(modes, base, zi, yi, wide, spread, second)
+    outs.append(local(second, out.at[:, 1], out_sems.at[4]))
+    outs[-1].start()
     for copy in outs:
         copy.wait()
 
@@ -548,28 +563,31 @@
     shape = jax.ShapeDtypeStruct
     deep = (X, 2, 4, 4, 2, C, 2 * K)
     lines = pltpu.VMEM((X, C, ROWS, 4 * K), BF)
-    wide = pltpu.VMEM((X, K * C, 2 * K), F32)
+    sample = pltpu.VMEM((C, ROWS, COLS), BF)
+    rows_wide = pltpu.VMEM((NG, C * G, COLS), F32)
+    wide = (K * C, 2 * K)
     table = pltpu.VMEM((COLS, COLS), BF)
     vmem = pltpu.VMEM
     dma = pltpu.SemaphoreType.DMA
     square = (C * G, C * G)
 
-    held, base, modes, grad_spec, zi, yi, small = pl.pallas_call(
+    held, first, base, modes, grad_spec, zi, yi, small = pl.pallas_call(
         main_kernel,
         out_shape=(
             grid_buffer(),
-            vmem((X, NG, C * G, COLS), F32),
-            vmem(deep, BF),
+            sample,
+            rows_wide,
+            vmem(deep[1:], BF),
             vmem((K // 2, 2 * C * C), F32),
             table,
             vmem((2 * ROWS, K), BF),
             vmem((16, 4 * C), F32),
         ),
         in_specs=[ANY] * 7 + [VMEM] * 4,
-        out_specs=[VMEM] * 7,
+        out_specs=[VMEM] * 8,
         scratch_shapes=[
-            grid_buffer(), grid_buffer(), lines, lines, grid_buffer(),
-            wide, vmem(deep, BF), vmem(deep, BF), vmem(deep, BF),
+            grid_buffer(), grid_buffer(), lines, lines, grid_buffer(), rows_wide,
+            vmem((X,) + wide, F32), vmem(deep, BF), vmem(deep, BF), vmem(deep, BF), vmem(deep, BF),
             table, vmem((K, 2 * ROWS), BF),
             vmem(square, BF), vmem(square, BF), vmem((C * G, 2 * K), F32), vmem(square, F32),
             vmem((C * G, COLS // 2), F32),
@@ -579,7 +597,7 @@
             exchange_scratch(), exchange_scratch(),
             dma((10,)), dma((2,)), [dma((3 + len(STEPS),)), dma((3 + len(STEPS),))],
         ],
-        compiler_params=params(46, 1),
+        compiler_params=params(51, 1),
         name="layer",
     )(
         field, cotangent, spec_weight, zf, zi, yf, yi,
@@ -595,12 +613,12 @@
             shape((C, C), F32),
             shape((1, C), F32),
         ),
-        in_specs=[VMEM] * 7,
+        in_specs=[VMEM] * 8,
         out_specs=[ANY] * 3 + [VMEM] * 2,
-        scratch_shapes=[lines, grid_buffer(), wide, dma((5,))],
+        scratch_shapes=[vmem((C, ROWS, 4 * K), BF), sample, vmem(wide, F32), dma((5,))],
         compiler_params=params(24),
         name="input_gradient",
-    )(held, base, modes, grad_spec, zi, yi, small)
+    )(held, first, base, modes, grad_spec, zi, yi, small)
 
     return output, grad_input, grad, term, total.reshape(C)
 

time: 74.9 us -> 76.3 us (1.019)
  Pallas kernels: 73.2 us -> 74.6 us
    pallas_call x1, Pallas kernels: 67.9 us -> 69.5 us  [local(): pl.pallas_call(main_kernel, out_shape=(grid_buffer(), sample, rows_wide,...]
where the time goes in v5:
time: 76.3 us; the launch traced here: 75.5 us
  Pallas kernels  74.6 us (98%)
  between operations  0.82 us (1%)
    pallas_call x1, Pallas kernels, local(): pl.pallas_call(main_kernel, out_shape=(grid_buffer(), sample, rows_wide,...  69.5 us
    pallas_call x1, Pallas kernels, local(): pl.pallas_call(last_kernel, out_shape=(shape(field.shape, BF), shape(fiel...  5.19 us

profile of v5, /device:TPU:0, one launch (start us, length us, event | category | flops | bytes accessed | tf_op | source)
XLA Modules:
  0.0 75.5 jit_solution(13205007136257426097)
XLA Ops:
  0.6 69.5 %layer.1 = (bf16[2,32,128,256]{3,2,1,0:T(8,128)(2,1)S(1)}, bf16[32,128,256]{2,1,0:T(8,128)(2,1)S(1)}, f32[8,512,256]{2,1,0:T(8,128)S(1)}, bf16[2,4,4,2,32,128]{5...) custom-call(bf16[32,2,128,256]{3,2,1,0:T(8,128)(2,1)} %field.1, ...), custom_call_target="tpu_custom_call" | custom-call | tf_op jit(solution)/shard_map/layer/pallas_call | solution.py:574
  70.1 5.2 %input_gradient.1 = (bf16[32,2,128,256]{3,2,1,0:T(8,128)(2,1)}, bf16[32,2,128,256]{3,2,1,0:T(8,128)(2,1)}, f32[32,2048]{1,0:T(8,128)}, f32[32,32]{1,0:T(8,128)}, f32[1,32]{1,0:T(1,128)}) custom-call(bf16[2,32,128,256]{3,2,1,0:T(8,128)(2,1)S(1)} %get-tuple-element.18.held, bf16[32,128,256]{2,1,0:T(8,128)(2,1)S(1)} %get-tuple-element.19.first, ...), custom_call_target="tpu_custom_call" | custom-call | tf_op jit(solution)/shard_map/input_gradient/pallas_call | solution.py:607

commit v6 on v5

--- a/solution.py
+++ b/solution.py
@@ -431,14 +431,14 @@
     bias_wide = jnp.broadcast_to(bias[...].astype(F32), (2 * K, C)).astype(BF)
     bias_col[...] = dot_nt(over, bias_wide)
     over_o, over_i = over_o_ref[...], over_i_ref[...]
-    arrived(f1)
-    f1 = scatter_rows(at, 1, part, b1)
     w_there.start()
     for load in loads[5:8]:
         load.start()
     pointwise(f_buf.at[0], kron, bias_col, base0)
     arrived(f0)
     f0 = scatter_halves(at, 0, b1)
+    arrived(f1)
+    f1 = scatter_rows(at, 1, part, b1)
     for load in loads[8:]:
         load.start()
     pointwise(f_buf.at[1], kron, bias_col, base1)
@@ -490,9 +490,9 @@
     ]
     arrived(f0)
     unmix(at, 0, scatter_total(at, 0, b2), w, over_o, over_i, modes2, dual)
+    arrived(f1)
+    f1 = scatter_halves(at, 1, b2)
     f0 = gather_rows(at, 0, modes2, b2)
-    arrived(f1)
-    f1 = scatter_halves(at, 1, b2)
     pointwise_back(g_buf.at[0], kron_back, base0)
     pointwise_back(g_buf.at[1], kron_back, base1)
     arrived(small)

time: 76.3 us -> 73.8 us (0.967)
  Pallas kernels: 74.6 us -> 72.1 us
    pallas_call x1, Pallas kernels: 69.5 us -> 66.9 us  [local(): pl.pallas_call(main_kernel, out_shape=(grid_buffer(), sample, rows_wide,...]
where the time goes in v6:
time: 73.8 us; the launch traced here: 72.9 us
  Pallas kernels  72.1 us (98%)
  between operations  0.82 us (1%)
    pallas_call x1, Pallas kernels, local(): pl.pallas_call(main_kernel, out_shape=(grid_buffer(), sample, rows_wide,...  66.9 us
    pallas_call x1, Pallas kernels, local(): pl.pallas_call(last_kernel, out_shape=(shape(field.shape, BF), shape(fiel...  5.19 us

profile of v6, /device:TPU:0, one launch (start us, length us, event | category | flops | bytes accessed | tf_op | source)
XLA Modules:
  0.0 72.9 jit_solution(3103090136462704698)
XLA Ops:
  0.6 66.9 %layer.1 = (bf16[2,32,128,256]{3,2,1,0:T(8,128)(2,1)S(1)}, bf16[32,128,256]{2,1,0:T(8,128)(2,1)S(1)}, f32[8,512,256]{2,1,0:T(8,128)S(1)}, bf16[2,4,4,2,32,128]{5...) custom-call(bf16[32,2,128,256]{3,2,1,0:T(8,128)(2,1)} %field.1, ...), custom_call_target="tpu_custom_call" | custom-call | tf_op jit(solution)/shard_map/layer/pallas_call | solution.py:574
  67.5 5.2 %input_gradient.1 = (bf16[32,2,128,256]{3,2,1,0:T(8,128)(2,1)}, bf16[32,2,128,256]{3,2,1,0:T(8,128)(2,1)}, f32[32,2048]{1,0:T(8,128)}, f32[32,32]{1,0:T(8,128)}, f32[1,32]{1,0:T(1,128)}) custom-call(bf16[2,32,128,256]{3,2,1,0:T(8,128)(2,1)S(1)} %get-tuple-element.18.held, bf16[32,128,256]{2,1,0:T(8,128)(2,1)S(1)} %get-tuple-element.19.first, ...), custom_call_target="tpu_custom_call" | custom-call | tf_op jit(solution)/shard_map/input_gradient/pallas_call | solution.py:607

commit v7 on v6

--- a/solution.py
+++ b/solution.py
@@ -452,32 +452,32 @@
     arrived(f1)
     f1 = scatter_halves(at, 1, b1)
     kron_back[...] = kron_of(dot_nt(over, point[...]), over, same)
+    f0 = gather_core(at, 0, modes, b1, f0)
     arrived(f1)
     mix(at, 1, scatter_total(at, 1, b1), w, over_o, over_i, modes, spec)
     f1 = gather_rows(at, 1, modes, b1)
-    f0 = gather_core(at, 0, modes, b1, f0)
 
     for load in loads[8:]:
         load.wait()
     arrived(f0)
     inverse_y(modes.at[0], yi, wide.at[0], spread.at[0])
     layer(spread.at[0], base0, c_buf.at[0], zi, zf, out.at[0], g_buf.at[0], rows.at[0])
-    f1 = gather_core(at, 1, modes, b1, f1)
     forward_y(rows.at[0], yf, wide.at[0], part2.at[0])
     f0 = scatter_core(at, 0, part2, b2)
+    f1 = gather_core(at, 1, modes, b1, f1)
+    arrived(f0)
+    f0 = scatter_rows(at, 0, part2, b2)
     arrived(f1)
     inverse_y(modes.at[1], yi, wide.at[1], spread.at[1])
-    arrived(f0)
-    f0 = scatter_rows(at, 0, part2, b2)
     layer(spread.at[1], base1, c_buf.at[1], zi, zf, out.at[1], g_buf.at[1], rows.at[1])
     forward_y(rows.at[1], yf, wide.at[1], part2.at[1])
     f1 = scatter_core(at, 1, part2, b2)
 
+    arrived(f1)
+    f1 = scatter_rows(at, 1, part2, b2)
+    arrived(f0)
+    f0 = scatter_halves(at, 0, b2)
     point_gradient(g_buf.at[0], f_buf.at[0], acc, bias_acc, True)
-    arrived(f1)
-    f1 = scatter_rows(at, 1, part2, b2)
-    arrived(f0)
-    f0 = scatter_halves(at, 0, b2)
     point_gradient(g_buf.at[1], f_buf.at[1], acc, bias_acc, False)
     same, over = group_masks()
     kept = jnp.where(same, acc[...], 0.0).reshape(C, G, C * G).sum(axis=1)
@@ -494,7 +494,6 @@
     f1 = scatter_halves(at, 1, b2)
     f0 = gather_rows(at, 0, modes2, b2)
     pointwise_back(g_buf.at[0], kron_back, base0)
-    pointwise_back(g_buf.at[1], kron_back, base1)
     arrived(small)
     s_small[1] = s_small[0] + r_small[0] + r_small[1] + r_small[2]
     arrived(f1)
@@ -505,6 +504,7 @@
         for n, step in enumerate(STEPS)
     ]
     weight_gradient(at, spec, dual, over_o, over_i, grad)
+    pointwise_back(g_buf.at[1], kron_back, base1)
     f0 = gather_core(at, 0, modes2, b2, f0)
     arrived(f0)
     input_gradient(modes2.at[0], base0, zi, yi, wide.at[0], spread.at[0], first)

time: 73.8 us -> 73.7 us (level)
  no operation moved by 1% of the time
where the time goes in v7:
time: 73.7 us; the launch traced here: 72.7 us
  Pallas kernels  71.8 us (97%)
  between operations  0.82 us (1%)
    pallas_call x1, Pallas kernels, local(): pl.pallas_call(main_kernel, out_shape=(grid_buffer(), sample, rows_wide,...  66.6 us
    pallas_call x1, Pallas kernels, local(): pl.pallas_call(last_kernel, out_shape=(shape(field.shape, BF), shape(fiel...  5.2 us

profile of v7, /device:TPU:0, one launch (start us, length us, event | category | flops | bytes accessed | tf_op | source)
XLA Modules:
  0.0 72.7 jit_solution(12945708289149176739)
XLA Ops:
  0.6 66.6 %layer.1 = (bf16[2,32,128,256]{3,2,1,0:T(8,128)(2,1)S(1)}, bf16[32,128,256]{2,1,0:T(8,128)(2,1)S(1)}, f32[8,512,256]{2,1,0:T(8,128)S(1)}, bf16[2,4,4,2,32,128]{5...) custom-call(bf16[32,2,128,256]{3,2,1,0:T(8,128)(2,1)} %field.1, ...), custom_call_target="tpu_custom_call" | custom-call | tf_op jit(solution)/shard_map/layer/pallas_call | solution.py:574
  67.3 5.2 %input_gradient.1 = (bf16[32,2,128,256]{3,2,1,0:T(8,128)(2,1)}, bf16[32,2,128,256]{3,2,1,0:T(8,128)(2,1)}, f32[32,2048]{1,0:T(8,128)}, f32[32,32]{1,0:T(8,128)}, f32[1,32]{1,0:T(1,128)}) custom-call(bf16[2,32,128,256]{3,2,1,0:T(8,128)(2,1)S(1)} %get-tuple-element.18.held, bf16[32,128,256]{2,1,0:T(8,128)(2,1)S(1)} %get-tuple-element.19.first, ...), custom_call_target="tpu_custom_call" | custom-call | tf_op jit(solution)/shard_map/input_gradient/pallas_call | solution.py:607
